TPU v7x, 512 devices: a whole 4x4x16 slice. The times are simulated.
512 devices in a mesh: section: 32 (over z_hi, y, core), tensor: 4 (over z_lo), dp: 4 (over x).
Axes of the slice: x: 4, y: 4, z: 16 (z_hi: 4, z_lo: 4; z = z_hi * 4 + z_lo), core: 2. Of those that a mesh axis runs over, the one named last changes fastest.
Arguments:
- image_rows: bfloat16 [4, 256, 7680], P('dp', 'section'), may hold values from -40 to 40, as said below
- key_weight: bfloat16 [32, 7680, 512], P('section', None, 'tensor'), may hold values from -0.0625 to 0.0625
- value_weight: bfloat16 [32, 7680, 512], P('section', None, 'tensor'), may hold values from -0.0625 to 0.0625
- key_gain: float32 [16, 128], replicated, may hold values from 0.1 to 1.9
- query_gain: float32 [16, 128], replicated, may hold values from 0.1 to 1.9
- queries: bfloat16 [4, 32, 256, 4096], P('dp', 'section', None, 'tensor'), may hold values from -40 to 40, as said below
- cotangent: bfloat16 [4, 32, 256, 4096], P('dp', 'section', None, 'tensor'), may hold values from -6 to 6
- text_doc: int32 [4, 256], P('dp'), may hold values from 0 to 7, never falling along the last dimension, each value on 1 to 128 neighbouring positions
- row_doc: int32 [4, 256], P('dp'), may hold values from 0 to 7, never falling along the last dimension, each value on 1 to 128 neighbouring positions
Outputs:
- grad_rows: bfloat16 [4, 256, 7680], P('dp', 'section', 'tensor')
- key_gain_grad: float32 [32, 128], P('section')
- query_gain_grad: float32 [32, 128], P('section')
Inputs may be any that keep to these rules, and one draw needn't show every extreme that they name: `image_rows`: real values of order one. `queries`: real values of order one.
All inputs are finite; a program needn't handle non-finite values.
Results may differ from a plain program's by a relative error of at most 0.024.
Values may be sent and summed in bfloat16 or wider, within the bound.
A program may use at most 64 MiB of HBM per device.

v0:
```python
import math

import jax
import jax.numpy as jnp
from jax import lax
from jax.sharding import PartitionSpec as P

HEAD = 128


EPSILON = 1e-05


def head_norm(inputs_raw, scaling):
    inverse_rms = lax.rsqrt(jnp.mean(inputs_raw * inputs_raw, axis=-1, keepdims=True) + EPSILON)
    normalized = inputs_raw * inverse_rms
    return (normalized, inverse_rms, normalized * scaling)


def norm_back(upstream, normalized, inverse_rms, scaling):
    scaled_up = upstream * scaling
    return inverse_rms * (
        scaled_up - normalized * jnp.mean(scaled_up * normalized, axis=-1, keepdims=True)
    )


def attend_back(queries_in, keys_in, values_in, upstream, allowed):
    tok_rows, query_heads, head_size = queries_in.shape
    key_heads = keys_in.shape[1]
    group_size = query_heads // key_heads
    factor = 1.0 / math.sqrt(head_size)
    query_grouped = queries_in.reshape(tok_rows, key_heads, group_size, head_size)
    upstream_grouped = upstream.reshape(tok_rows, key_heads, group_size, head_size)
    scores = (
        jnp.einsum("ikgd,jkd->kgij", query_grouped, keys_in, preferred_element_type=jnp.float32)
        * factor
    )
    exponents = jnp.where(allowed[None, None], jnp.exp(scores), 0.0)
    softmax = exponents / jnp.sum(exponents, axis=-1, keepdims=True)
    rounded = softmax.astype(jnp.bfloat16)
    grad_softmax = jnp.einsum(
        "ikgd,jkd->kgij", upstream_grouped, values_in, preferred_element_type=jnp.float32
    )
    inner_sum = jnp.sum(softmax * grad_softmax, axis=-1, keepdims=True)
    grad_scores = (softmax * (grad_softmax - inner_sum)).astype(jnp.bfloat16)
    grad_value = jnp.einsum(
        "kgij,ikgd->jkd", rounded, upstream_grouped, preferred_element_type=jnp.float32
    ).astype(jnp.bfloat16)
    grad_key = (
        jnp.einsum("kgij,ikgd->jkd", grad_scores, query_grouped, preferred_element_type=jnp.float32)
        * factor
    )
    grad_query = (
        jnp.einsum("kgij,jkd->ikgd", grad_scores, keys_in, preferred_element_type=jnp.float32)
        * factor
    )
    return (grad_query.reshape(tok_rows, query_heads, head_size), grad_key, grad_value)


def on_device(
    image_rows,
    key_weight,
    value_weight,
    key_gain,
    query_gain,
    queries,
    cotangent,
    text_doc,
    row_doc,
):
    rows_local = image_rows[0]
    key_matrix = key_weight[0]
    value_matrix = value_weight[0]
    kv_width = key_matrix.shape[1]
    layer_index = lax.axis_index("section") // 2
    key_scaling = lax.dynamic_index_in_dim(key_gain, layer_index, 0, keepdims=False)
    query_scaling = lax.dynamic_index_in_dim(query_gain, layer_index, 0, keepdims=False)
    row_block = lax.all_gather(rows_local, "section", axis=0, tiled=True)
    projected = jnp.concatenate(
        [
            jnp.dot(row_block, key_matrix, preferred_element_type=jnp.float32),
            jnp.dot(row_block, value_matrix, preferred_element_type=jnp.float32),
        ],
        axis=1,
    )
    total_rows = projected.shape[0]
    key_heads = kv_width // HEAD
    key_raw = projected[:, :kv_width].reshape(total_rows, key_heads, HEAD)
    values_all = projected[:, kv_width:].astype(jnp.bfloat16).reshape(total_rows, key_heads, HEAD)
    key_normed, key_scale, key_scaled = head_norm(key_raw, key_scaling)
    query_raw = queries[0, 0]
    tok_rows = query_raw.shape[0]
    query_heads = query_raw.shape[1] // HEAD
    query_normed, query_scale, query_scaled = head_norm(
        query_raw.astype(jnp.float32).reshape(tok_rows, query_heads, HEAD), query_scaling
    )
    allowed = text_doc[0][:, None] == row_doc[0][None, :]
    grad_query, grad_key, grad_value = attend_back(
        query_scaled.astype(jnp.bfloat16),
        key_scaled.astype(jnp.bfloat16),
        values_all,
        cotangent[0, 0].reshape(tok_rows, query_heads, HEAD),
        allowed,
    )
    gain_key, gain_query = lax.psum(
        (
            jnp.sum(grad_key * key_normed, axis=(0, 1)),
            jnp.sum(grad_query * query_normed, axis=(0, 1)),
        ),
        ("tensor", "dp"),
    )
    key_back = (
        norm_back(grad_key, key_normed, key_scale, key_scaling)
        .astype(jnp.bfloat16)
        .reshape(total_rows, kv_width)
    )
    value_back = grad_value.reshape(total_rows, kv_width)
    partial_rows = lax.dot_general(
        key_back, key_matrix, (((1,), (1,)), ((), ())), preferred_element_type=jnp.float32
    )
    partial_rows = partial_rows + lax.dot_general(
        value_back, value_matrix, (((1,), (1,)), ((), ())), preferred_element_type=jnp.float32
    )
    summed = lax.psum_scatter(
        partial_rows.astype(jnp.bfloat16).astype(jnp.float32).astype(jnp.bfloat16),
        "section",
        scatter_dimension=0,
        tiled=True,
    )
    shares = lax.psum_scatter(summed, "tensor", scatter_dimension=1, tiled=True).astype(jnp.float32)
    return (shares.astype(jnp.bfloat16)[None], gain_key[None], gain_query[None])


def solution(mesh):
    in_specs = (
        P("dp", "section", None),
        P("section", None, "tensor"),
        P("section", None, "tensor"),
        P(),
        P(),
        P("dp", "section", None, "tensor"),
        P("dp", "section", None, "tensor"),
        P("dp", None),
        P("dp", None),
    )
    out_specs = (P("dp", "section", "tensor"), P("section", None), P("section", None))
    return jax.shard_map(
        on_device, mesh=mesh, in_specs=in_specs, out_specs=out_specs, check_vma=False
    )
```

profile of v0, /device:TPU:1, one launch (start us, length us, event | category | flops | bytes accessed | tf_op | source)
XLA Modules:
  0.0 329.9 jit_solution(4240481431510444165)
XLA Ops:
  7.2 0.7 all-gather.3.cloned.1.call-update
  8.0 1.9 copy.33
  9.9 1.2 copy.19
  11.3 1.1 mul.152
  12.3 2.6 copy.20
  14.9 0.7 dynamic-slice_bitcast_fusion.1
  15.6 1.4 fusion.41
  17.0 0.9 copy.32
  17.9 0.7 broadcast_multiply_fusion.1
  18.7 92.0 %all-gather.3.cloned.1.call-done = bf16[1,256,7680]{2,1,0:T(8,128)(2,1)} async-done(((bf16[1,8,7680]{2,1,0:T(8,128)(2,1)}), bf16[1,256,7680]{2,1,0:T(8,128)(2,1)}) %all-gather.3.cloned.1.call-update) | async-done | bytes 3932176 | tf_op jit(solution)/shard_map/all_gather | solution.py:78
  110.8 4.2 %multiply_reduce_fusion.1 = (f32[256]{0:T(256)S(1)}, f32[256,128]{0,1:T(8,128)S(1)}) fusion(bf16[1,7680,128]{2,1,0:T(8,128)(2,1)} %param.10, bf16[1,256,7680]{2,1,0:T(8,128)(2,1)} %all-gather.3.cloned.1.call-done), kind=kOutput, calls=%fused_computation.51 | convolution fusion | flops 503381760 | bytes 6030336 | tf_op jit(solution)/shard_map/dot_general | solution.py:81
  115.0 2.1 fusion.14
  117.1 6.0 %fusion.5 = (f32[8,256]{1,0:T(8,128)S(1)}, f32[256,256,8]{1,0,2:T(8,128)}) fusion(f32[8,256]{1,0:T(8,128)S(1)} %get-tuple-element.11, f32[256,256,8]{1,0,2:T(8,128)} %get-tuple-element.12, pred[256,256]{0,1:T(8,128)(4,1)S(1)} %broadcast_compare_fusion, bf16[256,8,128]{2,1,0:T(8,128)(2,1)} %bitcast.161, bf16[1,7680,128]{2,1,0:T(8,128)(2,1)S(1)} %copy-done, ...), kind=kOutput, calls=%fused_computation.9 | convolution fusion | flops 640186368 | bytes 10698752 | tf_op jit(solution)/shard_map/ikgd,jkd->kgij/dot_general | solution.py:41
  123.2 2.8 fusion.34
  125.9 0.9 copy-done.1
  126.9 0.6 fusion.49
  127.9 4.4 %fusion.10 = f32[256,7680]{1,0:T(8,128)} fusion(bf16[1,7680,128]{2,1,0:T(8,128)(2,1)S(1)} %copy-done.2, f32[256,128]{0,1:T(8,128)S(1)} %get-tuple-element.10, f32[1,128,256]{2,1,0:T(8,128)S(1)} %get-tuple-element.15, f32[256]{0:T(256)S(1)} %broadcast_multiply_fusion, f32[128]{0:T(128)S(1)} %get-tuple-element.7, f32[256]{0:T(256)S(1)} %add_rsqrt_fusion.1), kind=kOutput, calls=%fused_computation.14 | convolution fusion | flops 503513088 | bytes 10095104 | tf_op jit(solution)/shard_map/dot_general | solution.py:118
  132.2 7.8 %fusion = bf16[256,7680]{1,0:T(8,128)(2,1)} fusion(f32[256,7680]{1,0:T(8,128)} %fusion.10, bf16[1,7680,128]{2,1,0:T(8,128)(2,1)S(1)} %copy-done, f32[256,256,8]{1,0,2:T(8,128)} %get-tuple-element.12, f32[8,256]{1,0:T(8,128)S(1)} %get-tuple-element.11, pred[256,256]{0,1:T(8,128)(4,1)S(1)} %broadcast_compare_fusion, bf16[256,8,128]{2,1,0:T(8,128)(2,1)} %bitcast.162), kind=kOutput, calls=%fused_computation.1 | convolution fusion | flops 643596288 | bytes 16457728 | tf_op jit(solution)/shard_map/dot_general | solution.py:121
  140.1 131.8 %reduce-scatter.5.cloned.1.call-done = bf16[8,7680]{1,0:T(8,128)(2,1)} async-done(((bf16[256,7680]{1,0:T(8,128)(2,1)}), bf16[8,7680]{1,0:T(8,128)(2,1)}) %reduce-scatter.5.cloned.1.call-update) | async-done | bytes 122896 | tf_op jit(solution)/shard_map/reduce_scatter | solution.py:124
  271.9 2.5 copy.30
  274.4 1.7 fusion.17
  276.1 35.1 %all-reduce = (f32[1,128]{1,0:T(1,128)}, f32[1,128]{1,0:T(1,128)}) all-reduce(f32[1,128]{1,0:T(1,128)S(1)} %bitcast.170, f32[1,128]{1,0:T(1,128)S(1)} %bitcast.169), channel_id=1, replica_groups=mesh['section'=32,'tensor'=4,'dp'=4] {'tensor','dp'}, use_global_device_ids=true, to_apply=%region_8.9 | all-reduce | flops 256 | bytes 2048 | tf_op jit(solution)/shard_map/psum | solution.py:105
  311.2 10.4 %reduce-scatter.7.cloned.1.call-done = bf16[1920,8]{1,0:T(8,128)(2,1)} async-done(((bf16[7680,8]{1,0:T(8,128)(2,1)}), bf16[1920,8]{1,0:T(8,128)(2,1)}) %reduce-scatter.7.cloned.1.call-update) | async-done | bytes 30736
  321.5 1.8 copy.31
  (24 shorter events, 0.8 us)
Async XLA Ops:
  7.2 110.0 %copy-start = (bf16[1,7680,128]{2,1,0:T(8,128)(2,1)S(1)}, bf16[1,7680,128]{2,1,0:T(8,128)(2,1)}, u32[]{:S(2)}) copy-start(bf16[1,7680,128]{2,1,0:T(8,128)(2,1)} %param.11) | copy-start | bytes 5898244
  7.2 103.6 %all-gather.3.cloned.1.call-start = ((), (), s32[]{:S(2)}) async-start(), calls=%async_computation.3 | async-start | bytes 4055040 | tf_op jit(solution)/shard_map/all_gather | solution.py:78
  7.9 264.0 %reduce-scatter.5.cloned.1.call-start = ((), (), s32[]{:S(2)}) async-start(), calls=%async_computation.2 | async-start | bytes 4055040 | tf_op jit(solution)/shard_map/reduce_scatter | solution.py:124
  11.2 4.5 %copy-start.3 = (bf16[1,1,256,1024]{3,2,1,0:T(8,128)(2,1)S(1)}, bf16[1,1,256,1024]{3,2,1,0:T(8,128)(2,1)}, u32[]{:S(2)}) copy-start(bf16[1,1,256,1024]{3,2,1,0:T(8,128)(2,1)} %param.14) | copy-start | bytes 1572868
  14.9 3.7 %copy-start.5 = (s32[1,256]{1,0:T(1,128)S(1)}, s32[1,256]{1,0:T(1,128)}, u32[]{:S(2)}) copy-start(s32[1,256]{1,0:T(1,128)} %param.16) | copy-start | bytes 3076
  14.9 3.7 %copy-start.6 = (s32[1,256]{1,0:T(1,128)S(1)}, s32[1,256]{1,0:T(1,128)}, u32[]{:S(2)}) copy-start(s32[1,256]{1,0:T(1,128)} %param.17) | copy-start | bytes 3076
  110.8 4.2 %copy-start.4 = (bf16[32,8,8,128]{3,2,1,0:T(8,128)(2,1)S(1)}, bf16[32,8,8,128]{3,2,1,0:T(8,128)(2,1)}, u32[]{:S(2)}) copy-start(bf16[32,8,8,128]{3,2,1,0:T(8,128)(2,1)} %copy.32) | copy-start | bytes 1572868
  125.9 1.0 copy-start.1
  125.9 1.9 copy-start.2
  140.0 181.5 %reduce-scatter.7.cloned.1.call-start = ((), (), s32[]{:S(2)}) async-start(), calls=%async_computation.4 | async-start | bytes 2457600
Sparse Core Ops, SparseCore 0:
  11.1 99.5 all-gather.2
  140.1 131.6 reduce-scatter.4
  274.7 46.7 reduce-scatter.6
where the time goes:
time: 330 us
  waiting for transfers between devices  235 us (71%)
  blocking collectives  35.1 us (11%)
  matrix products  26.7 us (8%)
  local copies, waits for them, and re-layouts  14.1 us (4%)
  between operations  13.9 us (4%)
  other arithmetic  5.05 us (2%)
    reduce_scatter x1, waiting for transfers between devices, on_device(): lax.psum_scatter(partial_rows.astype(jnp.bfloat16).astype(jnp.float32).as...  132 us
    all_gather x1, waiting for transfers between devices, on_device(): row_block = lax.all_gather(rows_local, 'section', axis=0, tiled=True)  92 us
    psum x1, blocking collectives, on_device(): lax.psum((jnp.sum(grad_key * key_normed, axis=(0, 1)), jnp.sum(grad_query...  35.1 us
    unnamed x4, waiting for transfers between devices  11.1 us
    unnamed x18, local copies, waits for them, and re-layouts  8.52 us
    dot_general x1, matrix products, on_device(): lax.dot_general(value_back, value_matrix, (((1,), (1,)), ((), ())), prefe...  7.77 us
  transfers between devices with their start and end apart: 3, of which 3 were waited for; matrix products, arithmetic and copies ran while one was open for 4% of the time, Pallas kernels for 0%

commit v1 on v0

v1 whole, which is shorter than its diff:
```python
import math

import jax
import jax.numpy as jnp
from jax import lax
from jax.experimental import pallas as pl
from jax.experimental.pallas import tpu as pltpu
from jax.sharding import PartitionSpec as P

HEAD = 128
EPSILON = 1e-05
MESH = pl.DeviceIdType.MESH
F32 = jnp.float32
BF16 = jnp.bfloat16
ROWS = 16


def kernel(
    x_ref, kw_ref, vw_ref, kg_ref, qg_ref, q_hbm, ct_hbm, td_ref, rd_ref,
    out_ref, gk_out, gq_out,
    wb, q_buf, ct_buf, qs_buf, qn_buf, xs, xr, g, raw, raw_send, raw_recv, kv, p,
    y1, y2, ysum, yred, zin, zred, zf, fs, fr, gain_a, gain_b, mask,
    w_sem, w_ss, w_rs, qc_sem, x_ss, x_rs, zo_ss, zf_ss, z_rs, ys_ss, y_rs, yf_ss, yf_rs,
    pr_ss, pr_rs, kv_ss, kv_rs, r1_ss, r1_rs, r2_ss, r2_rs, r3_ss, r3_rs,
    in_ss, in_rs, z4_ss, z4_rs, f_ss, f_rs, ga_ss, ga_rs, gb_ss, gb_rs,
):
    s = lax.axis_index("section")
    l = lax.axis_index("tensor")
    xi = lax.axis_index("dp")
    a = s // 8
    y = (s // 2) % 4
    c = s % 2
    half = g.shape[1]
    quarter = half // 2
    tok = q_buf.shape[0]
    heads = q_buf.shape[1] // HEAD
    rows = g.shape[0]
    block = 4 * ROWS
    layer = s // 2

    def dev(a_=None, y_=None, c_=None, l_=None, x_=None):
        a_ = a if a_ is None else lax.rem(a_ + 8, 4)
        y_ = y if y_ is None else lax.rem(y_ + 8, 4)
        c_ = c if c_ is None else c_
        return {
            "section": (a_ * 4 + y_) * 2 + c_,
            "tensor": l if l_ is None else l_,
            "dp": xi if x_ is None else x_,
        }

    def remote(src, dst, ss, rs, to):
        return pltpu.make_async_remote_copy(
            src_ref=src, dst_ref=dst, send_sem=ss, recv_sem=rs, device_id=to, device_id_type=MESH
        )

    partner = dev(c_=1 - c)
    edge = jnp.logical_or(l == 0, l == 3)
    even = lax.rem(l, 2) == 0
    mate = jnp.where(even, l + 1, l - 1)
    step = jnp.where(even, 1, -1)
    a_of = [a, lax.rem(a - step + 4, 4), lax.rem(a + step + 4, 4), lax.rem(a + 2, 4)]

    barrier = pltpu.get_barrier_semaphore()

    def greet(to):
        pl.semaphore_signal(barrier, inc=1, device_id=to, device_id_type=MESH)

    greet(partner)
    greet(dev(y_=y + 1))
    greet(dev(y_=y - 1))
    for d in range(1, 4):
        greet(dev(l_=lax.rem(l + d, 4)))
        greet(dev(a_=a + d))
        greet(dev(x_=lax.rem(xi + d, 4)))

    greet(dev(a_=a - step, l_=jnp.where(even, 3, 0)))

    @pl.when(edge)
    def _():
        greet(dev(a_=a + 2, l_=jnp.where(l == 0, 3, 0)))

    own_rows = pl.ds(pl.multiple_of(c * half, 128), half)
    their_rows = pl.ds(pl.multiple_of((1 - c) * half, 128), half)
    loads = [
        pltpu.make_async_copy(kw_ref.at[own_rows, :], wb.at[:, 0:HEAD], w_sem.at[0]),
        pltpu.make_async_copy(vw_ref.at[own_rows, :], wb.at[:, HEAD : 2 * HEAD], w_sem.at[1]),
        pltpu.make_async_copy(q_hbm, q_buf, qc_sem.at[0]),
        pltpu.make_async_copy(ct_hbm, ct_buf, qc_sem.at[1]),
    ]
    for copy in loads:
        copy.start()
    low = x_ref[:, :half].astype(F32)
    high = x_ref[:, half:].astype(F32)
    first = c == 0
    own = jnp.where(first, low, high)
    xs[...] = jnp.where(first, high, low)
    pl.semaphore_wait(barrier, 12 + jnp.where(edge, 3, 0))

    pending = []

    def send(copy, when=None):
        pending.append((when, copy))
        if when is None:
            copy.start()
        else:
            pl.when(when)(copy.start)

    send(remote(xs, xr, x_ss, x_rs, partner))
    x_copy = pending[-1][1]
    x_copy.wait_recv()
    got = xr[...]
    mine = pl.ds(pl.multiple_of((a * 4 + y) * ROWS, ROWS), ROWS)
    g[mine, :] = jnp.concatenate(
        [jnp.where(first, own, got), jnp.where(first, got, own)], axis=0
    ).astype(BF16)

    def shard(a_, y_, h):
        y_ = lax.rem(y_ + 8, 4)
        at = pl.ds(pl.multiple_of((a_ * 4 + y_) * ROWS, ROWS), ROWS)
        return g.at[at, h * quarter : (h + 1) * quarter]

    def y_send(k, h):
        piece = shard(a_of[k], y, h)
        send(remote(piece, piece, ys_ss.at[k, h, 0], y_rs.at[k, h, 0], dev(y_=y + 1)))
        send(remote(piece, piece, ys_ss.at[k, h, 1], y_rs.at[k, h, 1], dev(y_=y - 1)))

    def y_wait(k, h, side):
        piece = shard(a_of[k], y - 1 if side == 0 else y + 1, h)
        remote(piece, piece, ys_ss.at[k, h, side], y_rs.at[k, h, side], partner).wait_recv()

    def y_forward(k):
        for side in range(2):
            y_wait(k, side, side)
            piece = shard(a_of[k], y - 1 if side == 0 else y + 1, side)
            to = dev(y_=y + 1 if side == 0 else y - 1)
            send(remote(piece, piece, yf_ss.at[k, side], yf_rs.at[k, side], to))

    def y_finish(k):
        for side in range(2):
            y_wait(k, 1 - side, side)
        for side in range(2):
            piece = shard(a_of[k], y + 2, side)
            remote(piece, piece, yf_ss.at[k, side], yf_rs.at[k, side], partner).wait_recv()

    def z_wait(k, h):
        piece = shard(a_of[k], y, h)
        remote(piece, piece, zf_ss.at[0, h], z_rs.at[k, h], partner).wait_recv()

    last = l == 3
    far = jnp.where(last, 0, 3)
    side_a = jnp.where(last, a + 1, a - 1)
    targets = [
        (dev(a_=side_a, l_=far), 1),
        (dev(a_=side_a, l_=jnp.where(last, 2, 1)), 1),
        (dev(a_=a + 2, l_=far), 3),
    ]
    for h in range(2):
        piece = shard(a, y, h)
        to, k = targets[0]
        send(remote(piece, piece, zo_ss.at[0, h], z_rs.at[k, h], to), edge)
        y_send(0, h)
    for i in range(1, 3):
        for h in range(2):
            piece = shard(a, y, h)
            to, k = targets[i]
            send(remote(piece, piece, zo_ss.at[i, h], z_rs.at[k, h], to), edge)
    send(remote(kw_ref.at[their_rows, :], wb.at[:, 2 * HEAD : 3 * HEAD], w_ss.at[0], w_rs.at[0], partner))
    send(remote(vw_ref.at[their_rows, :], wb.at[:, 3 * HEAD : 4 * HEAD], w_ss.at[1], w_rs.at[1], partner))
    w_copies = [pending[-2][1], pending[-1][1]]

    loads[2].wait()
    q_gain = qg_ref[pl.ds(layer, 1), :]
    k_gain = kg_ref[pl.ds(layer, 1), :]

    def norm_queries(h, carry):
        at = pl.ds(pl.multiple_of(h * HEAD, HEAD), HEAD)
        raw_q = q_buf[:, at].astype(F32)
        scale = lax.rsqrt(jnp.mean(raw_q * raw_q, axis=-1, keepdims=True) + EPSILON)
        normed = raw_q * scale
        qn_buf[:, at] = normed
        qs_buf[:, at] = (normed * q_gain).astype(BF16)
        return carry

    lax.fori_loop(0, heads, norm_queries, 0)
    row_doc = jnp.broadcast_to(rd_ref[...].astype(F32), (rows, rows)).T
    mask[...] = jnp.where(row_doc == td_ref[...].astype(F32), 1.0, 0.0)

    y_forward(0)
    for h in range(2):
        z_wait(1, h)
        piece = shard(a_of[1], y, h)
        send(remote(piece, piece, zf_ss.at[0, h], z_rs.at[2, h], dev(l_=mate)))
        y_send(1, h)

    def project(k):
        y_finish(k)
        at = pl.ds(pl.multiple_of(a_of[k] * block, block), block)
        out = jnp.dot(g[at, :], wb[...], preferred_element_type=F32)
        raw[at, :] = out[:, : 2 * HEAD]
        raw_send[at, :] = out[:, 2 * HEAD :]
        send(remote(raw_send.at[at, :], raw_recv.at[at, :], pr_ss.at[k], pr_rs.at[k], partner))

    loads[0].wait()
    loads[1].wait()
    for copy in w_copies:
        copy.wait_recv()
    loads[3].wait()
    project(0)
    for h in range(2):
        z_wait(2, h)
        y_send(2, h)
    y_forward(1)
    for h in range(2):
        z_wait(3, h)
        piece = shard(a_of[3], y, h)
        send(remote(piece, piece, zf_ss.at[1, h], z_rs.at[3, h], dev(l_=mate)), edge)
        y_send(3, h)
    y_forward(2)
    project(1)
    y_forward(3)
    project(2)
    project(3)

    for k in range(4):
        at = pl.ds(pl.multiple_of(a_of[k] * block, block), block)
        remote(raw_send.at[at, :], raw_recv.at[at, :], pr_ss.at[k], pr_rs.at[k], partner).wait_recv()
    projected = raw[...] + raw_recv[...]
    key_raw = projected[:, :HEAD]
    values = projected[:, HEAD:].astype(BF16)
    key_scale = lax.rsqrt(jnp.mean(key_raw * key_raw, axis=-1, keepdims=True) + EPSILON)
    key_normed = key_raw * key_scale
    keys = (key_normed * k_gain).astype(BF16)
    factor = 1.0 / math.sqrt(HEAD)
    nt = (((1,), (1,)), ((), ()))
    tn = (((0,), (0,)), ((), ()))

    def head(h, carry):
        grad_key, grad_value, gain = carry
        at = pl.ds(pl.multiple_of(h * HEAD, HEAD), HEAD)
        query = qs_buf[:, at]
        upstream = ct_buf[:, at]
        scores = lax.dot_general(keys, query, nt, preferred_element_type=F32) * factor
        exponents = jnp.exp(scores) * mask[...]
        softmax = exponents * (1.0 / jnp.sum(exponents, axis=0, keepdims=True))
        grad_softmax = lax.dot_general(values, upstream, nt, preferred_element_type=F32)
        inner = jnp.sum(softmax * grad_softmax, axis=0, keepdims=True)
        grad_scores = (softmax * (grad_softmax - inner)).astype(BF16)
        grad_value = grad_value + jnp.dot(softmax.astype(BF16), upstream, preferred_element_type=F32)
        grad_key = grad_key + jnp.dot(grad_scores, query, preferred_element_type=F32)
        grad_query = lax.dot_general(grad_scores, keys, tn, preferred_element_type=F32)
        gain = gain + jnp.sum(grad_query * qn_buf[:, at], axis=0, keepdims=True)
        return grad_key, grad_value, gain

    zero = jnp.zeros((rows, HEAD), F32)
    grad_key, grad_value, gain_query = lax.fori_loop(
        0, heads, head, (zero, zero, jnp.zeros((1, HEAD), F32))
    )
    grad_key = grad_key * factor
    scaled_up = grad_key * k_gain
    key_back = key_scale * (
        scaled_up - key_normed * jnp.mean(scaled_up * key_normed, axis=-1, keepdims=True)
    )
    kv[:, :HEAD] = key_back.astype(BF16)
    kv[:, HEAD : 2 * HEAD] = grad_value.astype(BF16)
    kv_copy = remote(kv.at[:, : 2 * HEAD], kv.at[:, 2 * HEAD :], kv_ss, kv_rs, partner)
    send(kv_copy)

    gain_a[l] = jnp.concatenate(
        [
            jnp.sum(grad_key * key_normed, axis=0, keepdims=True),
            gain_query * factor,
            jnp.zeros((6, HEAD), F32),
        ],
        axis=0,
    )
    for d in range(1, 4):
        to = dev(l_=lax.rem(l + d, 4))
        send(remote(gain_a.at[l], gain_a.at[l], ga_ss.at[d - 1], ga_rs.at[d - 1], to))
    kv_copy.wait_recv()

    b_of = [lax.rem(a + 2, 4), lax.rem(a + 1, 4), lax.rem(a + 3, 4), a]
    y_up, y_down = dev(y_=y + 1), dev(y_=y - 1)

    def part(b, y_, h):
        y_ = lax.rem(y_ + 8, 4)
        at = pl.ds(pl.multiple_of((b * 4 + y_) * ROWS, ROWS), ROWS)
        return p.at[at, h * quarter : (h + 1) * quarter]

    def terms(k):
        b = b_of[k]
        at = pl.ds(pl.multiple_of(b * block, block), block)
        left = kv[at, :]
        for h in range(2):
            cols = slice(h * quarter, (h + 1) * quarter)
            p[at, cols] = lax.dot_general(
                left, wb[cols, :], nt, preferred_element_type=F32
            ).astype(BF16)
            send(remote(part(b, y + 2, h), y1.at[h, k], r1_ss.at[h, k], r1_rs.at[h, k], y_up if h == 0 else y_down))
        for h in range(2):
            src = part(b, y + 1, 1) if h == 0 else part(b, y - 1, 0)
            dst = y2.at[h, k, 1 - h]
            send(remote(src, dst, r2_ss.at[h, k], r2_rs.at[h, k], y_up if h == 0 else y_down))

    def pass_on(k):
        b = b_of[k]
        for h in range(2):
            remote(y1.at[h, k], y1.at[h, k], r1_ss.at[h, k], r1_rs.at[h, k], partner).wait_recv()
            mine_ = part(b, y + 1, 0) if h == 0 else part(b, y - 1, 1)
            ysum[h, k] = (mine_[...].astype(F32) + y1[h, k].astype(F32)).astype(BF16)
            send(remote(ysum.at[h, k], y2.at[h, k, h], r3_ss.at[h, k], r3_rs.at[h, k], y_up if h == 0 else y_down))

    active = c == l // 2

    def group(k):
        b = b_of[k]
        for h in range(2):
            remote(y2.at[h, k, 1 - h], y2.at[h, k, 1 - h], r2_ss.at[h, k], r2_rs.at[h, k], partner).wait_recv()
            remote(y2.at[h, k, h], y2.at[h, k, h], r3_ss.at[h, k], r3_rs.at[h, k], partner).wait_recv()
        for i in range(2):
            yred[k, i] = (
                part(b, y, i)[...].astype(F32) + y2[0, k, i].astype(F32) + y2[1, k, i].astype(F32)
            ).astype(BF16)
            to = 2 * c + i
            slot = lax.rem(l - to + 4, 4)
            slot_ = jnp.maximum(slot - 1, 0)
            send(
                remote(yred.at[k, i], zin.at[k, slot_], in_ss.at[k, i], in_rs.at[k, slot_], dev(l_=to)),
                to != l,
            )

    def group_sum(k):
        for d in range(3):
            remote(zin.at[k, d], zin.at[k, d], in_ss.at[k, 0], in_rs.at[k, d], partner).wait_recv()
        total = jnp.where(even, yred[k, 0].astype(F32), yred[k, 1].astype(F32))
        for d in range(3):
            total = total + zin[k, d].astype(F32)
        return total

    def across(k):
        @pl.when(active)
        def _():
            zred[k] = group_sum(k).astype(BF16)
            z4_copy(k).start()

    def z4_copy(k):
        return remote(zred.at[k], zf.at[k], z4_ss.at[k], z4_rs.at[k], dev(a_=b_of[k]))

    terms(0)
    terms(1)
    pass_on(0)
    terms(2)
    pass_on(1)
    terms(3)

    for d in range(1, 4):
        src = gain_a.at[lax.rem(l - d + 4, 4)]
        remote(src, src, ga_ss.at[d - 1], ga_rs.at[d - 1], partner).wait_recv()
    gain_b[xi] = gain_a[0] + gain_a[1] + gain_a[2] + gain_a[3]
    for d in range(1, 4):
        to = dev(x_=lax.rem(xi + d, 4))
        send(remote(gain_b.at[xi], gain_b.at[xi], gb_ss.at[d - 1], gb_rs.at[d - 1], to))

    group(0)
    pass_on(2)
    group(1)
    across(0)
    pass_on(3)
    group(2)
    across(1)
    group(3)
    across(2)

    for d in range(1, 4):
        src = gain_b.at[lax.rem(xi - d + 4, 4)]
        remote(src, src, gb_ss.at[d - 1], gb_rs.at[d - 1], partner).wait_recv()
    gains = gain_b[0] + gain_b[1] + gain_b[2] + gain_b[3]
    gk_out[...] = gains[0:1]
    gq_out[...] = gains[1:2]

    f_copy = remote(fs, fr, f_ss, f_rs, partner)

    @pl.when(active)
    def _():
        total = group_sum(3)
        for k in range(3):
            z4_copy(k).wait_recv()
            total = total + zf[k].astype(F32)
        top, bottom = total[: ROWS // 2], total[ROWS // 2 :]
        fs[...] = jnp.where(first, bottom, top)
        f_copy.start()
        out_ref[...] = jnp.where(first, top, bottom).astype(BF16)
        for k in range(3):
            z4_copy(k).wait_send()
        f_copy.wait_send()

    @pl.when(jnp.logical_not(active))
    def _():
        f_copy.wait_recv()
        out_ref[...] = fr[...].astype(BF16)

    for when, copy in pending:
        if when is None:
            copy.wait_send()
        else:
            pl.when(when)(copy.wait_send)


def on_device(
    image_rows,
    key_weight,
    value_weight,
    key_gain,
    query_gain,
    queries,
    cotangent,
    text_doc,
    row_doc,
):
    width = image_rows.shape[2]
    half = width // 2
    quarter = half // 2
    tok = queries.shape[2]
    q_width = queries.shape[3]
    rows = row_doc.shape[1]
    vmem = pl.BlockSpec(memory_space=pltpu.VMEM)
    anywhere = pl.BlockSpec(memory_space=pl.ANY)
    dma = pltpu.SemaphoreType.DMA
    scratch = [
        pltpu.VMEM((half, 4 * HEAD), BF16),
        pltpu.VMEM((tok, q_width), BF16),
        pltpu.VMEM((tok, q_width), BF16),
        pltpu.VMEM((tok, q_width), BF16),
        pltpu.VMEM((tok, q_width), F32),
        pltpu.VMEM((8, half), F32),
        pltpu.VMEM((8, half), F32),
        pltpu.VMEM((rows, half), BF16),
        pltpu.VMEM((rows, 2 * HEAD), F32),
        pltpu.VMEM((rows, 2 * HEAD), F32),
        pltpu.VMEM((rows, 2 * HEAD), F32),
        pltpu.VMEM((rows, 4 * HEAD), BF16),
        pltpu.VMEM((rows, half), BF16),
        pltpu.VMEM((2, 4, ROWS, quarter), BF16),
        pltpu.VMEM((2, 4, 2, ROWS, quarter), BF16),
        pltpu.VMEM((2, 4, ROWS, quarter), BF16),
        pltpu.VMEM((4, 2, ROWS, quarter), BF16),
        pltpu.VMEM((4, 3, ROWS, quarter), BF16),
        pltpu.VMEM((3, ROWS, quarter), BF16),
        pltpu.VMEM((3, ROWS, quarter), BF16),
        pltpu.VMEM((8, quarter), F32),
        pltpu.VMEM((8, quarter), F32),
        pltpu.VMEM((4, 8, HEAD), F32),
        pltpu.VMEM((4, 8, HEAD), F32),
        pltpu.VMEM((rows, tok), F32),
        dma((2,)), dma((2,)), dma((2,)), dma((2,)), dma, dma,
        dma((3, 2)), dma((2, 2)), dma((4, 2)),
        dma((4, 2, 2)), dma((4, 2, 2)), dma((4, 2)), dma((4, 2)),
        dma((4,)), dma((4,)), dma, dma,
        dma((2, 4)), dma((2, 4)), dma((2, 4)), dma((2, 4)), dma((2, 4)), dma((2, 4)),
        dma((4, 2)), dma((4, 3)), dma((3,)), dma((3,)), dma, dma,
        dma((3,)), dma((3,)), dma((3,)), dma((3,)),
    ]
    grad, gain_key, gain_query = pl.pallas_call(
        kernel,
        name="image_row_gradients",
        out_shape=(
            jax.ShapeDtypeStruct((8, quarter), BF16),
            jax.ShapeDtypeStruct((1, HEAD), F32),
            jax.ShapeDtypeStruct((1, HEAD), F32),
        ),
        in_specs=[vmem, anywhere, anywhere, vmem, vmem, anywhere, anywhere, vmem, vmem],
        out_specs=(vmem, vmem, vmem),
        scratch_shapes=scratch,
        compiler_params=pltpu.CompilerParams(
            collective_id=0, has_side_effects=True, vmem_limit_bytes=48 * 1024 * 1024
        ),
    )(
        image_rows[0], key_weight[0], value_weight[0], key_gain, query_gain,
        queries[0, 0], cotangent[0, 0], text_doc, row_doc,
    )
    return (grad[None], gain_key, gain_query)


def solution(mesh):
    in_specs = (
        P("dp", "section", None),
        P("section", None, "tensor"),
        P("section", None, "tensor"),
        P(),
        P(),
        P("dp", "section", None, "tensor"),
        P("dp", "section", None, "tensor"),
        P("dp", None),
        P("dp", None),
    )
    out_specs = (P("dp", "section", "tensor"), P("section", None), P("section", None))
    return jax.shard_map(
        on_device, mesh=mesh, in_specs=in_specs, out_specs=out_specs, check_vma=False
    )
```

time: 330 us -> 97.2 us (0.29)
  waiting for transfers between devices: 235 us -> 0 us
  Pallas kernels: 0 us -> 84.7 us
  blocking collectives: 35.1 us -> 0 us
  matrix products: 26.7 us -> 0 us
  between operations: 13.9 us -> 0.66 us
  other arithmetic: 5.05 us -> 0 us
  local copies, waits for them, and re-layouts: 14.1 us -> 10.4 us
    reduce_scatter x1 -> x0, waiting for transfers between devices: 132 us -> none  [on_device(): lax.psum_scatter(partial_rows.astype(jnp.bfloat16).astype(jnp.float32).as...]
    all_gather x1 -> x0, waiting for transfers between devices: 92 us -> none  [on_device(): row_block = lax.all_gather(rows_local, 'section', axis=0, tiled=True)]
    pallas_call x0 -> x1, Pallas kernels: none -> 84.7 us  [on_device(): pl.pallas_call(kernel, name='image_row_gradients', out_shape=(jax.ShapeDt...]
    psum x1 -> x0, blocking collectives: 35.1 us -> none  [on_device(): lax.psum((jnp.sum(grad_key * key_normed, axis=(0, 1)), jnp.sum(grad_query...]
    dot_general x7 -> x0, matrix products: 26.7 us -> none  [the longest x1 7.77 us: on_device(): lax.dot_general(value_back, value_matrix, (((1,), (1,)), ((), ())), prefe...]
    unnamed x4 -> x0, waiting for transfers between devices: 11.1 us -> none
    mul x4 -> x0, local copies, waits for them, and re-layouts: 4.34 us -> none  [the longest x2 3.62 us: head_norm(): normalized = inputs_raw * inverse_rms]
    unnamed x18 -> x21, local copies, waits for them, and re-layouts: 8.52 us -> 10.4 us
  transfers between devices with their start and end apart: 3 -> 0, of which waited for: 3 -> 0; matrix products, arithmetic and copies ran while one was open for 4% -> 0% of each run, Pallas kernels for 0% -> 0%
where the time goes in v1:
time: 97.2 us; the launch traced here: 95.8 us
  Pallas kernels  84.7 us (87%)
  local copies, waits for them, and re-layouts  10.4 us (11%)
    pallas_call x1, Pallas kernels, on_device(): pl.pallas_call(kernel, name='image_row_gradients', out_shape=(jax.ShapeDt...  84.7 us
    unnamed x21, local copies, waits for them, and re-layouts  10.4 us

profile of v1, /device:TPU:1, one launch (start us, length us, event | category | flops | bytes accessed | tf_op | source)
XLA Modules:
  0.0 95.8 jit_solution(8446296710382081510)
XLA Ops:
  0.6 0.0 copy-start
  0.6 1.5 %copy-done = bf16[1,7680,128]{2,1,0:T(8,128)(2,1)S(1)} copy-done((bf16[1,7680,128]{2,1,0:T(8,128)(2,1)S(1)}, bf16[1,7680,128]{2,1,0:T(8,128)(2,1)}, u32[]{:S(2)}) %copy-start) | copy-done | bytes 1966104
  2.2 0.0 copy-start.1
  2.2 1.5 %copy-done.1 = bf16[1,7680,128]{2,1,0:T(8,128)(2,1)S(1)} copy-done((bf16[1,7680,128]{2,1,0:T(8,128)(2,1)S(1)}, bf16[1,7680,128]{2,1,0:T(8,128)(2,1)}, u32[]{:S(2)}) %copy-start.1) | copy-done | bytes 1966104
  3.7 0.0 copy-start.2
  3.7 1.0 %copy-done.2 = bf16[1,1,256,1024]{3,2,1,0:T(8,128)(2,1)S(1)} copy-done((bf16[1,1,256,1024]{3,2,1,0:T(8,128)(2,1)S(1)}, bf16[1,1,256,1024]{3,2,1,0:T(8,128)(2,1)}, u32[]{:S(2)}) %copy-start.2) | copy-done | bytes 524312
  4.8 0.0 copy-start.3
  4.8 1.0 %copy-done.3 = bf16[1,1,256,1024]{3,2,1,0:T(8,128)(2,1)S(1)} copy-done((bf16[1,1,256,1024]{3,2,1,0:T(8,128)(2,1)S(1)}, bf16[1,1,256,1024]{3,2,1,0:T(8,128)(2,1)}, u32[]{:S(2)}) %copy-start.3) | copy-done | bytes 524312
  5.8 0.0 copy-start.4
  5.8 0.9 copy-done.4
  6.7 0.0 copy-start.5
  6.7 0.7 copy-done.5
  7.4 0.0 copy-start.6
  7.4 0.7 copy-done.6
  8.1 0.0 copy-start.7
  8.1 0.7 copy-done.7
  8.8 0.0 copy-start.8
  8.8 0.7 copy-done.8
  9.5 84.7 %image_row_gradients.1 = (bf16[8,1920]{1,0:T(8,128)(2,1)S(1)}, f32[1,128]{1,0:T(1,128)S(1)}, f32[1,128]{1,0:T(1,128)S(1)}) custom-call(bf16[8,7680]{1,0:T(8,128)(2,1)S(1)} %bitcast.10, bf16[7680,128]{1,0:T(8,128)(2,1)S(1)} %bitcast.6, bf16[7680,128]{1,0:T(8,128)(2,1)S(1)} %bitcast.7, f32[16,128]{1,0:T(8,128)S(1)} %copy-done.5, f32[16,128]{1,0:T(8,128)S(1)} %copy-done.6, ...), custom_call_target="tpu_custom_call" | custom-call | tf_op jit(solution)/shard_map/image_row_gradients/pallas_call | solution.py:462
  94.2 0.6 copy.15
  94.8 0.5 copy.16
  95.3 0.5 copy.17
Async XLA Ops:
  0.6 1.5 %copy-start = (bf16[1,7680,128]{2,1,0:T(8,128)(2,1)S(1)}, bf16[1,7680,128]{2,1,0:T(8,128)(2,1)}, u32[]{:S(2)}) copy-start(bf16[1,7680,128]{2,1,0:T(8,128)(2,1)} %param.10) | copy-start | bytes 5898244
  2.2 1.5 %copy-start.1 = (bf16[1,7680,128]{2,1,0:T(8,128)(2,1)S(1)}, bf16[1,7680,128]{2,1,0:T(8,128)(2,1)}, u32[]{:S(2)}) copy-start(bf16[1,7680,128]{2,1,0:T(8,128)(2,1)} %param.11) | copy-start | bytes 5898244
  3.7 1.0 %copy-start.2 = (bf16[1,1,256,1024]{3,2,1,0:T(8,128)(2,1)S(1)}, bf16[1,1,256,1024]{3,2,1,0:T(8,128)(2,1)}, u32[]{:S(2)}) copy-start(bf16[1,1,256,1024]{3,2,1,0:T(8,128)(2,1)} %param.14) | copy-start | bytes 1572868
  4.8 1.0 %copy-start.3 = (bf16[1,1,256,1024]{3,2,1,0:T(8,128)(2,1)S(1)}, bf16[1,1,256,1024]{3,2,1,0:T(8,128)(2,1)}, u32[]{:S(2)}) copy-start(bf16[1,1,256,1024]{3,2,1,0:T(8,128)(2,1)} %param.15) | copy-start | bytes 1572868
  5.8 0.9 copy-start.4
  6.7 0.7 copy-start.5
  7.4 0.7 copy-start.6
  8.1 0.7 copy-start.7
  8.8 0.7 copy-start.8

commit v2 on v1

--- a/solution.py
+++ b/solution.py
@@ -16,11 +16,12 @@
 
 
 def kernel(
-    x_ref, kw_ref, vw_ref, kg_ref, qg_ref, q_hbm, ct_hbm, td_ref, rd_ref,
+    x_hbm, kw_ref, vw_ref, kg_hbm, qg_hbm, q_hbm, ct_hbm, td_hbm, rd_hbm,
     out_ref, gk_out, gq_out,
+    x_ref, kg_ref, qg_ref, td_ref, rd_ref,
     wb, q_buf, ct_buf, qs_buf, qn_buf, xs, xr, g, raw, raw_send, raw_recv, kv, p,
     y1, y2, ysum, yred, zin, zred, zf, fs, fr, gain_a, gain_b, mask,
-    w_sem, w_ss, w_rs, qc_sem, x_ss, x_rs, zo_ss, zf_ss, z_rs, ys_ss, y_rs, yf_ss, yf_rs,
+    s_sem, w_sem, w_ss, w_rs, qc_sem, x_ss, x_rs, zo_ss, zf_ss, z_rs, ys_ss, y_rs, yf_ss, yf_rs,
     pr_ss, pr_rs, kv_ss, kv_rs, r1_ss, r1_rs, r2_ss, r2_rs, r3_ss, r3_rs,
     in_ss, in_rs, z4_ss, z4_rs, f_ss, f_rs, ga_ss, ga_rs, gb_ss, gb_rs,
 ):
@@ -60,6 +61,15 @@
     step = jnp.where(even, 1, -1)
     a_of = [a, lax.rem(a - step + 4, 4), lax.rem(a + step + 4, 4), lax.rem(a + 2, 4)]
 
+    small = [
+        pltpu.make_async_copy(src, dst, s_sem.at[i])
+        for i, (src, dst) in enumerate(
+            [(x_hbm, x_ref), (kg_hbm, kg_ref), (qg_hbm, qg_ref), (td_hbm, td_ref), (rd_hbm, rd_ref)]
+        )
+    ]
+    for copy in small:
+        copy.start()
+
     barrier = pltpu.get_barrier_semaphore()
 
     def greet(to):
@@ -70,14 +80,9 @@
     greet(dev(y_=y - 1))
     for d in range(1, 4):
         greet(dev(l_=lax.rem(l + d, 4)))
-        greet(dev(a_=a + d))
         greet(dev(x_=lax.rem(xi + d, 4)))
 
     greet(dev(a_=a - step, l_=jnp.where(even, 3, 0)))
-
-    @pl.when(edge)
-    def _():
-        greet(dev(a_=a + 2, l_=jnp.where(l == 0, 3, 0)))
 
     own_rows = pl.ds(pl.multiple_of(c * half, 128), half)
     their_rows = pl.ds(pl.multiple_of((1 - c) * half, 128), half)
@@ -89,12 +94,14 @@
     ]
     for copy in loads:
         copy.start()
+    for copy in small:
+        copy.wait()
     low = x_ref[:, :half].astype(F32)
     high = x_ref[:, half:].astype(F32)
     first = c == 0
     own = jnp.where(first, low, high)
     xs[...] = jnp.where(first, high, low)
-    pl.semaphore_wait(barrier, 12 + jnp.where(edge, 3, 0))
+    pl.semaphore_wait(barrier, 9 + jnp.where(edge, 2, 0))
 
     pending = []
 
@@ -149,21 +156,17 @@
     last = l == 3
     far = jnp.where(last, 0, 3)
     side_a = jnp.where(last, a + 1, a - 1)
-    targets = [
-        (dev(a_=side_a, l_=far), 1),
-        (dev(a_=side_a, l_=jnp.where(last, 2, 1)), 1),
-        (dev(a_=a + 2, l_=far), 3),
-    ]
+    beyond = dev(a_=side_a, l_=far)
+    targets = [(beyond, 1), (dev(a_=side_a, l_=jnp.where(last, 2, 1)), 1)]
     for h in range(2):
         piece = shard(a, y, h)
         to, k = targets[0]
         send(remote(piece, piece, zo_ss.at[0, h], z_rs.at[k, h], to), edge)
         y_send(0, h)
-    for i in range(1, 3):
-        for h in range(2):
-            piece = shard(a, y, h)
-            to, k = targets[i]
-            send(remote(piece, piece, zo_ss.at[i, h], z_rs.at[k, h], to), edge)
+    for h in range(2):
+        piece = shard(a, y, h)
+        to, k = targets[1]
+        send(remote(piece, piece, zo_ss.at[1, h], z_rs.at[k, h], to), edge)
     send(remote(kw_ref.at[their_rows, :], wb.at[:, 2 * HEAD : 3 * HEAD], w_ss.at[0], w_rs.at[0], partner))
     send(remote(vw_ref.at[their_rows, :], wb.at[:, 3 * HEAD : 4 * HEAD], w_ss.at[1], w_rs.at[1], partner))
     w_copies = [pending[-2][1], pending[-1][1]]
@@ -208,6 +211,8 @@
     project(0)
     for h in range(2):
         z_wait(2, h)
+        piece = shard(a_of[2], y, h)
+        send(remote(piece, piece, zo_ss.at[2, h], z_rs.at[3, h], beyond), edge)
         y_send(2, h)
     y_forward(1)
     for h in range(2):
@@ -295,7 +300,14 @@
             p[at, cols] = lax.dot_general(
                 left, wb[cols, :], nt, preferred_element_type=F32
             ).astype(BF16)
+
+    def opposite(k):
+        b = b_of[k]
+        for h in range(2):
             send(remote(part(b, y + 2, h), y1.at[h, k], r1_ss.at[h, k], r1_rs.at[h, k], y_up if h == 0 else y_down))
+
+    def beside(k):
+        b = b_of[k]
         for h in range(2):
             src = part(b, y + 1, 1) if h == 0 else part(b, y - 1, 0)
             dst = y2.at[h, k, 1 - h]
@@ -346,11 +358,18 @@
         return remote(zred.at[k], zf.at[k], z4_ss.at[k], z4_rs.at[k], dev(a_=b_of[k]))
 
     terms(0)
+    opposite(0)
+    beside(0)
     terms(1)
+    opposite(1)
     pass_on(0)
+    beside(1)
     terms(2)
+    opposite(2)
     pass_on(1)
+    beside(2)
     terms(3)
+    opposite(3)
 
     for d in range(1, 4):
         src = gain_a.at[lax.rem(l - d + 4, 4)]
@@ -362,6 +381,7 @@
 
     group(0)
     pass_on(2)
+    beside(3)
     group(1)
     across(0)
     pass_on(3)
@@ -423,9 +443,14 @@
     q_width = queries.shape[3]
     rows = row_doc.shape[1]
     vmem = pl.BlockSpec(memory_space=pltpu.VMEM)
-    anywhere = pl.BlockSpec(memory_space=pl.ANY)
+    hbm = pl.BlockSpec(memory_space=pltpu.HBM)
     dma = pltpu.SemaphoreType.DMA
     scratch = [
+        pltpu.VMEM((8, width), BF16),
+        pltpu.VMEM(key_gain.shape, F32),
+        pltpu.VMEM(query_gain.shape, F32),
+        pltpu.VMEM(text_doc.shape, jnp.int32),
+        pltpu.VMEM(row_doc.shape, jnp.int32),
         pltpu.VMEM((half, 4 * HEAD), BF16),
         pltpu.VMEM((tok, q_width), BF16),
         pltpu.VMEM((tok, q_width), BF16),
@@ -451,7 +476,7 @@
         pltpu.VMEM((4, 8, HEAD), F32),
         pltpu.VMEM((4, 8, HEAD), F32),
         pltpu.VMEM((rows, tok), F32),
-        dma((2,)), dma((2,)), dma((2,)), dma((2,)), dma, dma,
+        dma((5,)), dma((2,)), dma((2,)), dma((2,)), dma((2,)), dma, dma,
         dma((3, 2)), dma((2, 2)), dma((4, 2)),
         dma((4, 2, 2)), dma((4, 2, 2)), dma((4, 2)), dma((4, 2)),
         dma((4,)), dma((4,)), dma, dma,
@@ -467,11 +492,11 @@
             jax.ShapeDtypeStruct((1, HEAD), F32),
             jax.ShapeDtypeStruct((1, HEAD), F32),
         ),
-        in_specs=[vmem, anywhere, anywhere, vmem, vmem, anywhere, anywhere, vmem, vmem],
+        in_specs=[hbm] * 9,
         out_specs=(vmem, vmem, vmem),
         scratch_shapes=scratch,
         compiler_params=pltpu.CompilerParams(
-            collective_id=0, has_side_effects=True, vmem_limit_bytes=48 * 1024 * 1024
+            collective_id=0, has_side_effects=True, vmem_limit_bytes=62 * 1024 * 1024
         ),
     )(
         image_rows[0], key_weight[0], value_weight[0], key_gain, query_gain,

time: 97.2 us -> 86.6 us (0.89)
  local copies, waits for them, and re-layouts: 10.4 us -> 3.69 us
  Pallas kernels: 84.7 us -> 81.6 us
    unnamed x21 -> x3, local copies, waits for them, and re-layouts: 10.4 us -> 3.69 us
    pallas_call x1, Pallas kernels: 84.7 us -> 81.6 us  [on_device(): pl.pallas_call(kernel, name='image_row_gradients', out_shape=(jax.ShapeDt...]
where the time goes in v2:
time: 86.6 us; the launch traced here: 86 us
  Pallas kernels  81.6 us (94%)
  local copies, waits for them, and re-layouts  3.69 us (4%)
    pallas_call x1, Pallas kernels, on_device(): pl.pallas_call(kernel, name='image_row_gradients', out_shape=(jax.ShapeDt...  81.6 us
    unnamed x3, local copies, waits for them, and re-layouts  3.69 us

profile of v2, /device:TPU:1, one launch (start us, length us, event | category | flops | bytes accessed | tf_op | source)
XLA Modules:
  0.0 86.0 jit_solution(15283597460474427584)
XLA Ops:
  0.6 81.6 %image_row_gradients.1 = (bf16[8,1920]{1,0:T(8,128)(2,1)}, f32[1,128]{1,0:T(1,128)}, f32[1,128]{1,0:T(1,128)}) custom-call(bf16[8,7680]{1,0:T(8,128)(2,1)} %bitcast.10, bf16[7680,128]{1,0:T(8,128)(2,1)} %bitcast.6, bf16[7680,128]{1,0:T(8,128)(2,1)} %bitcast.7, f32[16,128]{1,0:T(8,128)} %kg_hbm.1, f32[16,128]{1,0:T(8,128)} %qg_hbm.1, ...), custom_call_target="tpu_custom_call" | custom-call | tf_op jit(solution)/shard_map/image_row_gradients/pallas_call | solution.py:487
  82.3 1.4 %copy.15 = bf16[1,8,1920]{2,1,0:T(8,128)(2,1)} copy(bf16[1,8,1920]{2,1,0:T(8,128)(2,1)} %bitcast.11) | data formatting | bytes 61440
  83.6 1.2 %copy.16 = f32[1,128]{1,0:T(1,128)} copy(f32[1,128]{1,0:T(1,128)} %get-tuple-element.13) | data formatting | bytes 1024
  84.8 1.1 %copy.17 = f32[1,128]{1,0:T(1,128)} copy(f32[1,128]{1,0:T(1,128)} %get-tuple-element.14) | data formatting | bytes 1024

commit v3 on v2

--- a/solution.py
+++ b/solution.py
@@ -19,11 +19,11 @@
     x_hbm, kw_ref, vw_ref, kg_hbm, qg_hbm, q_hbm, ct_hbm, td_hbm, rd_hbm,
     out_ref, gk_out, gq_out,
     x_ref, kg_ref, qg_ref, td_ref, rd_ref,
-    wb, q_buf, ct_buf, qs_buf, qn_buf, xs, xr, g, raw, raw_send, raw_recv, kv, p,
-    y1, y2, ysum, yred, zin, zred, zf, fs, fr, gain_a, gain_b, mask,
-    s_sem, w_sem, w_ss, w_rs, qc_sem, x_ss, x_rs, zo_ss, zf_ss, z_rs, ys_ss, y_rs, yf_ss, yf_rs,
+    wb, wm, q_buf, ct_buf, qs_buf, qn_buf, xs, xr, g, raw, raw_send, raw_recv, kv, p,
+    y1, y2, ysum, yred, zin, fs, fr, gain_a, gain_b, mask,
+    s_sem, w_sem, w_ss, w_rs, wz_ss, wz_rs, wx_ss, wx_rs, wf_ss, wf_rs, qc_sem, x_ss, x_rs, zo_ss, zf_ss, z_rs, ys_ss, y_rs, yf_ss, yf_rs,
     pr_ss, pr_rs, kv_ss, kv_rs, r1_ss, r1_rs, r2_ss, r2_rs, r3_ss, r3_rs,
-    in_ss, in_rs, z4_ss, z4_rs, f_ss, f_rs, ga_ss, ga_rs, gb_ss, gb_rs,
+    in_ss, in_rs, f_ss, f_rs, ga_ss, ga_rs, gb_ss, gb_rs,
 ):
     s = lax.axis_index("section")
     l = lax.axis_index("tensor")
@@ -82,6 +82,7 @@
         greet(dev(l_=lax.rem(l + d, 4)))
         greet(dev(x_=lax.rem(xi + d, 4)))
 
+    greet(dev(l_=mate, c_=1 - c))
     greet(dev(a_=a - step, l_=jnp.where(even, 3, 0)))
 
     own_rows = pl.ds(pl.multiple_of(c * half, 128), half)
@@ -101,7 +102,7 @@
     first = c == 0
     own = jnp.where(first, low, high)
     xs[...] = jnp.where(first, high, low)
-    pl.semaphore_wait(barrier, 9 + jnp.where(edge, 2, 0))
+    pl.semaphore_wait(barrier, 10 + jnp.where(edge, 2, 0))
 
     pending = []
 
@@ -112,6 +113,49 @@
         else:
             pl.when(when)(copy.start)
 
+    share = quarter // 4
+
+    def to_mate(i):
+        core = c if i == 0 else 1 - c
+        start = (2 * core + lax.rem(mate, 2)) * quarter + xi * share
+        src_rows = pl.ds(pl.multiple_of(start, ROWS), share)
+        dst_rows = pl.ds(pl.multiple_of(xi * share, ROWS), share)
+        for j, ref in enumerate((kw_ref, vw_ref)):
+            n = 2 * i + j
+            dst = wm.at[dst_rows, n * HEAD : (n + 1) * HEAD]
+            send(remote(ref.at[src_rows, :], dst, wz_ss.at[n], wz_rs.at[n], dev(l_=mate, c_=core)))
+
+    def piece_of(x_, i):
+        at = pl.ds(pl.multiple_of(lax.rem(x_ + 4, 4) * share, ROWS), share)
+        return wm.at[at, 2 * i * HEAD : 2 * (i + 1) * HEAD]
+
+    x_up, x_down = dev(x_=lax.rem(xi + 1, 4)), dev(x_=lax.rem(xi + 3, 4))
+
+    def to_dp(i):
+        for n in (2 * i, 2 * i + 1):
+            at = pl.ds(pl.multiple_of(xi * share, ROWS), share)
+            dst = wm.at[at, n * HEAD : (n + 1) * HEAD]
+            remote(dst, dst, wz_ss.at[n], wz_rs.at[n], partner).wait_recv()
+        own_piece = piece_of(xi, i)
+        send(remote(own_piece, own_piece, wx_ss.at[i, 0], wx_rs.at[i, 0], x_up))
+        send(remote(own_piece, own_piece, wx_ss.at[i, 1], wx_rs.at[i, 1], x_down))
+
+    def dp_wait(i, side):
+        part_ = piece_of(xi - 1 if side == 0 else xi + 1, i)
+        remote(part_, part_, wx_ss.at[i, side], wx_rs.at[i, side], partner).wait_recv()
+
+    def dp_forward(i):
+        dp_wait(i, i)
+        part_ = piece_of(xi - 1 if i == 0 else xi + 1, i)
+        send(remote(part_, part_, wf_ss.at[i], wf_rs.at[i], x_up if i == 0 else x_down))
+
+    def dp_finish():
+        for i in range(2):
+            dp_wait(i, 1 - i)
+            part_ = piece_of(xi + 2, i)
+            remote(part_, part_, wf_ss.at[i], wf_rs.at[i], partner).wait_recv()
+
+    to_mate(0)
     send(remote(xs, xr, x_ss, x_rs, partner))
     x_copy = pending[-1][1]
     x_copy.wait_recv()
@@ -170,6 +214,7 @@
     send(remote(kw_ref.at[their_rows, :], wb.at[:, 2 * HEAD : 3 * HEAD], w_ss.at[0], w_rs.at[0], partner))
     send(remote(vw_ref.at[their_rows, :], wb.at[:, 3 * HEAD : 4 * HEAD], w_ss.at[1], w_rs.at[1], partner))
     w_copies = [pending[-2][1], pending[-1][1]]
+    to_mate(1)
 
     loads[2].wait()
     q_gain = qg_ref[pl.ds(layer, 1), :]
@@ -203,6 +248,7 @@
         raw_send[at, :] = out[:, 2 * HEAD :]
         send(remote(raw_send.at[at, :], raw_recv.at[at, :], pr_ss.at[k], pr_rs.at[k], partner))
 
+    to_dp(0)
     loads[0].wait()
     loads[1].wait()
     for copy in w_copies:
@@ -215,14 +261,17 @@
         send(remote(piece, piece, zo_ss.at[2, h], z_rs.at[3, h], beyond), edge)
         y_send(2, h)
     y_forward(1)
+    to_dp(1)
     for h in range(2):
         z_wait(3, h)
         piece = shard(a_of[3], y, h)
         send(remote(piece, piece, zf_ss.at[1, h], z_rs.at[3, h], dev(l_=mate)), edge)
         y_send(3, h)
     y_forward(2)
+    dp_forward(0)
     project(1)
     y_forward(3)
+    dp_forward(1)
     project(2)
     project(3)
 
@@ -258,7 +307,7 @@
 
     zero = jnp.zeros((rows, HEAD), F32)
     grad_key, grad_value, gain_query = lax.fori_loop(
-        0, heads, head, (zero, zero, jnp.zeros((1, HEAD), F32))
+        0, heads, head, (zero, zero, jnp.zeros((1, HEAD), F32)), unroll=4
     )
     grad_key = grad_key * factor
     scaled_up = grad_key * k_gain
@@ -267,8 +316,17 @@
     )
     kv[:, :HEAD] = key_back.astype(BF16)
     kv[:, HEAD : 2 * HEAD] = grad_value.astype(BF16)
-    kv_copy = remote(kv.at[:, : 2 * HEAD], kv.at[:, 2 * HEAD :], kv_ss, kv_rs, partner)
-    send(kv_copy)
+    b_of = [lax.rem(a + 2, 4), lax.rem(a + 1, 4), lax.rem(a + 3, 4), a]
+    kv_to = [partner, dev(l_=mate), dev(l_=mate, c_=1 - c)]
+
+    def kv_copy(k, i):
+        at = pl.ds(pl.multiple_of(b_of[k] * block, block), block)
+        dst = kv.at[at, 2 * (i + 1) * HEAD : 2 * (i + 2) * HEAD]
+        return remote(kv.at[at, : 2 * HEAD], dst, kv_ss.at[k, i], kv_rs.at[k, i], kv_to[i])
+
+    for k in range(4):
+        for i in range(3):
+            send(kv_copy(k, i))
 
     gain_a[l] = jnp.concatenate(
         [
@@ -281,82 +339,69 @@
     for d in range(1, 4):
         to = dev(l_=lax.rem(l + d, 4))
         send(remote(gain_a.at[l], gain_a.at[l], ga_ss.at[d - 1], ga_rs.at[d - 1], to))
-    kv_copy.wait_recv()
-
-    b_of = [lax.rem(a + 2, 4), lax.rem(a + 1, 4), lax.rem(a + 3, 4), a]
+
     y_up, y_down = dev(y_=y + 1), dev(y_=y - 1)
-
-    def part(b, y_, h):
+    split = quarter // 2 // HEAD * HEAD + HEAD
+    cols = [slice(0, split), slice(split, quarter)]
+    width = [split, quarter - split]
+    w_rows = pl.ds(pl.multiple_of(lax.rem(l, 2) * quarter, ROWS), quarter)
+
+    def part(b, y_, h=None):
         y_ = lax.rem(y_ + 8, 4)
         at = pl.ds(pl.multiple_of((b * 4 + y_) * ROWS, ROWS), ROWS)
-        return p.at[at, h * quarter : (h + 1) * quarter]
+        return p.at[at, :] if h is None else p.at[at, cols[h]]
+
+    def y1_at(h, k):
+        return y1.at[h, k, :, : width[h]]
 
     def terms(k):
-        b = b_of[k]
-        at = pl.ds(pl.multiple_of(b * block, block), block)
-        left = kv[at, :]
-        for h in range(2):
-            cols = slice(h * quarter, (h + 1) * quarter)
-            p[at, cols] = lax.dot_general(
-                left, wb[cols, :], nt, preferred_element_type=F32
-            ).astype(BF16)
+        for i in range(3):
+            kv_copy(k, i).wait_recv()
+        at = pl.ds(pl.multiple_of(b_of[k] * block, block), block)
+        p[at, :] = (
+            lax.dot_general(kv[at, : 4 * HEAD], wb[w_rows, :], nt, preferred_element_type=F32)
+            + lax.dot_general(kv[at, 4 * HEAD :], wm[...], nt, preferred_element_type=F32)
+        ).astype(BF16)
 
     def opposite(k):
         b = b_of[k]
         for h in range(2):
-            send(remote(part(b, y + 2, h), y1.at[h, k], r1_ss.at[h, k], r1_rs.at[h, k], y_up if h == 0 else y_down))
+            send(remote(part(b, y + 2, h), y1_at(h, k), r1_ss.at[h, k], r1_rs.at[h, k], y_up if h == 0 else y_down))
 
     def beside(k):
         b = b_of[k]
         for h in range(2):
             src = part(b, y + 1, 1) if h == 0 else part(b, y - 1, 0)
-            dst = y2.at[h, k, 1 - h]
+            dst = y2.at[h, k, :, cols[1 - h]]
             send(remote(src, dst, r2_ss.at[h, k], r2_rs.at[h, k], y_up if h == 0 else y_down))
 
     def pass_on(k):
         b = b_of[k]
         for h in range(2):
-            remote(y1.at[h, k], y1.at[h, k], r1_ss.at[h, k], r1_rs.at[h, k], partner).wait_recv()
+            remote(y1_at(h, k), y1_at(h, k), r1_ss.at[h, k], r1_rs.at[h, k], partner).wait_recv()
             mine_ = part(b, y + 1, 0) if h == 0 else part(b, y - 1, 1)
-            ysum[h, k] = (mine_[...].astype(F32) + y1[h, k].astype(F32)).astype(BF16)
-            send(remote(ysum.at[h, k], y2.at[h, k, h], r3_ss.at[h, k], r3_rs.at[h, k], y_up if h == 0 else y_down))
+            total = ysum.at[h, k, :, : width[h]]
+            total[...] = (mine_[...].astype(F32) + y1_at(h, k)[...].astype(F32)).astype(BF16)
+            send(remote(total, y2.at[h, k, :, cols[h]], r3_ss.at[h, k], r3_rs.at[h, k], y_up if h == 0 else y_down))
 
     active = c == l // 2
+
+    owner = jnp.where(active, l, lax.rem(l + 2, 4))
+    slot = jnp.where(active, 0, 1)
 
     def group(k):
         b = b_of[k]
         for h in range(2):
-            remote(y2.at[h, k, 1 - h], y2.at[h, k, 1 - h], r2_ss.at[h, k], r2_rs.at[h, k], partner).wait_recv()
-            remote(y2.at[h, k, h], y2.at[h, k, h], r3_ss.at[h, k], r3_rs.at[h, k], partner).wait_recv()
-        for i in range(2):
-            yred[k, i] = (
-                part(b, y, i)[...].astype(F32) + y2[0, k, i].astype(F32) + y2[1, k, i].astype(F32)
-            ).astype(BF16)
-            to = 2 * c + i
-            slot = lax.rem(l - to + 4, 4)
-            slot_ = jnp.maximum(slot - 1, 0)
-            send(
-                remote(yred.at[k, i], zin.at[k, slot_], in_ss.at[k, i], in_rs.at[k, slot_], dev(l_=to)),
-                to != l,
-            )
-
-    def group_sum(k):
-        for d in range(3):
-            remote(zin.at[k, d], zin.at[k, d], in_ss.at[k, 0], in_rs.at[k, d], partner).wait_recv()
-        total = jnp.where(even, yred[k, 0].astype(F32), yred[k, 1].astype(F32))
-        for d in range(3):
-            total = total + zin[k, d].astype(F32)
-        return total
-
-    def across(k):
-        @pl.when(active)
-        def _():
-            zred[k] = group_sum(k).astype(BF16)
-            z4_copy(k).start()
-
-    def z4_copy(k):
-        return remote(zred.at[k], zf.at[k], z4_ss.at[k], z4_rs.at[k], dev(a_=b_of[k]))
-
+            for sem_s, sem_r, i in ((r2_ss, r2_rs, 1 - h), (r3_ss, r3_rs, h)):
+                dst = y2.at[h, k, :, cols[i]]
+                remote(dst, dst, sem_s.at[h, k], sem_r.at[h, k], partner).wait_recv()
+        total = part(b, y)[...].astype(F32) + y2[0, k].astype(F32) + y2[1, k].astype(F32)
+        yred[k] = total.astype(BF16)
+        to = dev(a_=b, l_=owner)
+        copy = remote(yred.at[k], zin.at[k, slot], in_ss.at[k], in_rs.at[k, slot], to)
+        send(copy, jnp.logical_not(active) if k == 3 else None)
+
+    dp_finish()
     terms(0)
     opposite(0)
     beside(0)
@@ -383,12 +428,9 @@
     pass_on(2)
     beside(3)
     group(1)
-    across(0)
     pass_on(3)
     group(2)
-    across(1)
     group(3)
-    across(2)
 
     for d in range(1, 4):
         src = gain_b.at[lax.rem(xi - d + 4, 4)]
@@ -401,16 +443,16 @@
 
     @pl.when(active)
     def _():
-        total = group_sum(3)
-        for k in range(3):
-            z4_copy(k).wait_recv()
-            total = total + zf[k].astype(F32)
+        total = yred[3].astype(F32)
+        for k in range(4):
+            for j in range(1 if k == 3 else 0, 2):
+                got_ = zin.at[k, j]
+                remote(got_, got_, in_ss.at[k], in_rs.at[k, j], partner).wait_recv()
+                total = total + got_[...].astype(F32)
         top, bottom = total[: ROWS // 2], total[ROWS // 2 :]
         fs[...] = jnp.where(first, bottom, top)
         f_copy.start()
         out_ref[...] = jnp.where(first, top, bottom).astype(BF16)
-        for k in range(3):
-            z4_copy(k).wait_send()
         f_copy.wait_send()
 
     @pl.when(jnp.logical_not(active))
@@ -423,6 +465,17 @@
             copy.wait_send()
         else:
             pl.when(when)(copy.wait_send)
+
+
+def hand_over(a_ref, b_ref, c_ref, a_out, b_out, c_out, sems):
+    copies = [
+        pltpu.make_async_copy(src, dst, sems.at[i])
+        for i, (src, dst) in enumerate([(a_ref, a_out), (b_ref, b_out), (c_ref, c_out)])
+    ]
+    for copy in copies:
+        copy.start()
+    for copy in copies:
+        copy.wait()
 
 
 def on_device(
@@ -452,6 +505,7 @@
         pltpu.VMEM(text_doc.shape, jnp.int32),
         pltpu.VMEM(row_doc.shape, jnp.int32),
         pltpu.VMEM((half, 4 * HEAD), BF16),
+        pltpu.VMEM((quarter, 4 * HEAD), BF16),
         pltpu.VMEM((tok, q_width), BF16),
         pltpu.VMEM((tok, q_width), BF16),
         pltpu.VMEM((tok, q_width), BF16),
@@ -462,26 +516,26 @@
         pltpu.VMEM((rows, 2 * HEAD), F32),
         pltpu.VMEM((rows, 2 * HEAD), F32),
         pltpu.VMEM((rows, 2 * HEAD), F32),
-        pltpu.VMEM((rows, 4 * HEAD), BF16),
-        pltpu.VMEM((rows, half), BF16),
+        pltpu.VMEM((rows, 8 * HEAD), BF16),
+        pltpu.VMEM((rows, quarter), BF16),
         pltpu.VMEM((2, 4, ROWS, quarter), BF16),
-        pltpu.VMEM((2, 4, 2, ROWS, quarter), BF16),
         pltpu.VMEM((2, 4, ROWS, quarter), BF16),
+        pltpu.VMEM((2, 4, ROWS, quarter), BF16),
+        pltpu.VMEM((4, ROWS, quarter), BF16),
         pltpu.VMEM((4, 2, ROWS, quarter), BF16),
-        pltpu.VMEM((4, 3, ROWS, quarter), BF16),
-        pltpu.VMEM((3, ROWS, quarter), BF16),
-        pltpu.VMEM((3, ROWS, quarter), BF16),
         pltpu.VMEM((8, quarter), F32),
         pltpu.VMEM((8, quarter), F32),
         pltpu.VMEM((4, 8, HEAD), F32),
         pltpu.VMEM((4, 8, HEAD), F32),
         pltpu.VMEM((rows, tok), F32),
-        dma((5,)), dma((2,)), dma((2,)), dma((2,)), dma((2,)), dma, dma,
+        dma((5,)), dma((2,)), dma((2,)), dma((2,)),
+        dma((4,)), dma((4,)), dma((2, 2)), dma((2, 2)), dma((2,)), dma((2,)),
+        dma((2,)), dma, dma,
         dma((3, 2)), dma((2, 2)), dma((4, 2)),
         dma((4, 2, 2)), dma((4, 2, 2)), dma((4, 2)), dma((4, 2)),
-        dma((4,)), dma((4,)), dma, dma,
+        dma((4,)), dma((4,)), dma((4, 3)), dma((4, 3)),
         dma((2, 4)), dma((2, 4)), dma((2, 4)), dma((2, 4)), dma((2, 4)), dma((2, 4)),
-        dma((4, 2)), dma((4, 3)), dma((3,)), dma((3,)), dma, dma,
+        dma((4,)), dma((4, 2)), dma, dma,
         dma((3,)), dma((3,)), dma((3,)), dma((3,)),
     ]
     grad, gain_key, gain_query = pl.pallas_call(
@@ -502,7 +556,20 @@
         image_rows[0], key_weight[0], value_weight[0], key_gain, query_gain,
         queries[0, 0], cotangent[0, 0], text_doc, row_doc,
     )
-    return (grad[None], gain_key, gain_query)
+    anywhere = pl.BlockSpec(memory_space=pl.ANY)
+    return pl.pallas_call(
+        hand_over,
+        name="hand_over",
+        out_shape=(
+            jax.ShapeDtypeStruct((1, 8, quarter), BF16),
+            jax.ShapeDtypeStruct((1, HEAD), F32),
+            jax.ShapeDtypeStruct((1, HEAD), F32),
+        ),
+        in_specs=[anywhere] * 3,
+        out_specs=(anywhere,) * 3,
+        scratch_shapes=[dma((3,))],
+        compiler_params=pltpu.CompilerParams(vmem_limit_bytes=62 * 1024 * 1024),
+    )(grad[None], gain_key, gain_query)
 
 
 def solution(mesh):

time: 86.6 us -> 79.2 us (0.915)
  local copies, waits for them, and re-layouts: 3.69 us -> 0 us
  Pallas kernels: 81.6 us -> 78.3 us
    pallas_call x1, Pallas kernels: 81.6 us -> 76.3 us  [on_device(): pl.pallas_call(kernel, name='image_row_gradients', out_shape=(jax.ShapeDt...]
    unnamed x3 -> x0, local copies, waits for them, and re-layouts: 3.69 us -> none
    pallas_call x0 -> x1, Pallas kernels: none -> 2.09 us  [on_device(): pl.pallas_call(hand_over, name='hand_over', out_shape=(jax.ShapeDtypeStru...]
where the time goes in v3:
time: 79.2 us; the launch traced here: 79 us
  Pallas kernels  78.3 us (99%)
    pallas_call x1, Pallas kernels, on_device(): pl.pallas_call(kernel, name='image_row_gradients', out_shape=(jax.ShapeDt...  76.3 us
    pallas_call x1, Pallas kernels, on_device(): pl.pallas_call(hand_over, name='hand_over', out_shape=(jax.ShapeDtypeStru...  2.09 us

profile of v3, /device:TPU:1, one launch (start us, length us, event | category | flops | bytes accessed | tf_op | source)
XLA Modules:
  0.0 79.0 jit_solution(16547194334127090003)
XLA Ops:
  0.6 76.3 %image_row_gradients.1 = (bf16[8,1920]{1,0:T(8,128)(2,1)}, f32[1,128]{1,0:T(1,128)}, f32[1,128]{1,0:T(1,128)}) custom-call(bf16[8,7680]{1,0:T(8,128)(2,1)} %bitcast.10, bf16[7680,128]{1,0:T(8,128)(2,1)} %bitcast.6, bf16[7680,128]{1,0:T(8,128)(2,1)} %bitcast.7, f32[16,128]{1,0:T(8,128)} %kg_hbm.1, f32[16,128]{1,0:T(8,128)} %qg_hbm.1, ...), custom_call_target="tpu_custom_call" | custom-call | tf_op jit(solution)/shard_map/image_row_gradients/pallas_call | solution.py:541
  76.9 2.1 %hand_over.1 = (bf16[1,8,1920]{2,1,0:T(8,128)(2,1)}, f32[1,128]{1,0:T(1,128)}, f32[1,128]{1,0:T(1,128)}) custom-call(bf16[1,8,1920]{2,1,0:T(8,128)(2,1)} %bitcast.11, f32[1,128]{1,0:T(1,128)} %get-tuple-element.7.b_ref, f32[1,128]{1,0:T(1,128)} %get-tuple-element.8.c_ref), custom_call_target="tpu_custom_call" | custom-call | tf_op jit(solution)/shard_map/hand_over/pallas_call | solution.py:560

commit v4 on v3

--- a/solution.py
+++ b/solution.py
@@ -19,7 +19,8 @@
     x_hbm, kw_ref, vw_ref, kg_hbm, qg_hbm, q_hbm, ct_hbm, td_hbm, rd_hbm,
     out_ref, gk_out, gq_out,
     x_ref, kg_ref, qg_ref, td_ref, rd_ref,
-    wb, wm, q_buf, ct_buf, qs_buf, qn_buf, xs, xr, g, raw, raw_send, raw_recv, kv, p,
+    wb, wm, q_buf, ct_buf, qs_buf, qn_buf, xs, xr,
+    e_buf, g_buf, gs_buf, sums, kn_buf, ks_buf, key_buf, g, raw, raw_send, raw_recv, kv, p,
     y1, y2, ysum, yred, zin, fs, fr, gain_a, gain_b, mask,
     s_sem, w_sem, w_ss, w_rs, wz_ss, wz_rs, wx_ss, wx_rs, wf_ss, wf_rs, qc_sem, x_ss, x_rs, zo_ss, zf_ss, z_rs, ys_ss, y_rs, yf_ss, yf_rs,
     pr_ss, pr_rs, kv_ss, kv_rs, r1_ss, r1_rs, r2_ss, r2_rs, r3_ss, r3_rs,
@@ -33,8 +34,9 @@
     c = s % 2
     half = g.shape[1]
     quarter = half // 2
-    tok = q_buf.shape[0]
-    heads = q_buf.shape[1] // HEAD
+    heads = q_hbm.shape[1] // HEAD
+    tok = q_hbm.shape[0]
+    group_cols = 2 * tok
     rows = g.shape[0]
     block = 4 * ROWS
     layer = s // 2
@@ -90,9 +92,13 @@
     loads = [
         pltpu.make_async_copy(kw_ref.at[own_rows, :], wb.at[:, 0:HEAD], w_sem.at[0]),
         pltpu.make_async_copy(vw_ref.at[own_rows, :], wb.at[:, HEAD : 2 * HEAD], w_sem.at[1]),
-        pltpu.make_async_copy(q_hbm, q_buf, qc_sem.at[0]),
-        pltpu.make_async_copy(ct_hbm, ct_buf, qc_sem.at[1]),
     ]
+    for h in range(heads):
+        for i, (src, dst) in enumerate(((q_hbm, q_buf), (ct_hbm, ct_buf))):
+            there = dst.at[h * tok : (h + 1) * tok, :]
+            loads.append(
+                pltpu.make_async_copy(src.at[:, h * HEAD : (h + 1) * HEAD], there, qc_sem.at[i, h])
+            )
     for copy in loads:
         copy.start()
     for copy in small:
@@ -216,22 +222,25 @@
     w_copies = [pending[-2][1], pending[-1][1]]
     to_mate(1)
 
-    loads[2].wait()
+    for copy in loads[2:]:
+        copy.wait()
     q_gain = qg_ref[pl.ds(layer, 1), :]
     k_gain = kg_ref[pl.ds(layer, 1), :]
 
     def norm_queries(h, carry):
-        at = pl.ds(pl.multiple_of(h * HEAD, HEAD), HEAD)
-        raw_q = q_buf[:, at].astype(F32)
+        at = pl.ds(pl.multiple_of(h * tok, tok), tok)
+        raw_q = q_buf[at, :].astype(F32)
         scale = lax.rsqrt(jnp.mean(raw_q * raw_q, axis=-1, keepdims=True) + EPSILON)
         normed = raw_q * scale
-        qn_buf[:, at] = normed
-        qs_buf[:, at] = (normed * q_gain).astype(BF16)
+        qn_buf[at, :] = normed
+        qs_buf[at, :] = (normed * q_gain).astype(BF16)
         return carry
 
     lax.fori_loop(0, heads, norm_queries, 0)
     row_doc = jnp.broadcast_to(rd_ref[...].astype(F32), (rows, rows)).T
-    mask[...] = jnp.where(row_doc == td_ref[...].astype(F32), 1.0, 0.0)
+    allowed = jnp.where(row_doc == td_ref[...].astype(F32), 1.0, 0.0)
+    mask[:, :tok] = allowed
+    mask[:, tok:] = allowed
 
     y_forward(0)
     for h in range(2):
@@ -248,12 +257,46 @@
         raw_send[at, :] = out[:, 2 * HEAD :]
         send(remote(raw_send.at[at, :], raw_recv.at[at, :], pr_ss.at[k], pr_rs.at[k], partner))
 
+    factor = 1.0 / math.sqrt(HEAD)
+    nt = (((1,), (1,)), ((), ()))
+    tn = (((0,), (0,)), ((), ()))
+    groups = range(0, heads * tok, group_cols)
+
+    def scores_of(k):
+        at = pl.ds(pl.multiple_of(a_of[k] * block, block), block)
+        remote(raw_send.at[at, :], raw_recv.at[at, :], pr_ss.at[k], pr_rs.at[k], partner).wait_recv()
+        projected = raw[at, :] + raw_recv[at, :]
+        key_raw = projected[:, :HEAD]
+        values = projected[:, HEAD:].astype(BF16)
+        key_scale = lax.rsqrt(jnp.mean(key_raw * key_raw, axis=-1, keepdims=True) + EPSILON)
+        key_normed = key_raw * key_scale
+        keys = (key_normed * k_gain).astype(BF16)
+        ks_buf[at, :] = jnp.broadcast_to(key_scale, key_raw.shape)
+        kn_buf[at, :] = key_normed
+        key_buf[at, :] = keys
+        for start in groups:
+            here = slice(start, start + group_cols)
+            scores = lax.dot_general(keys, qs_buf[here, :], nt, preferred_element_type=F32)
+            exponents = jnp.exp(scores * factor) * mask[at, :]
+            grad_softmax = lax.dot_general(values, ct_buf[here, :], nt, preferred_element_type=F32)
+            e_buf[at, here] = exponents
+            g_buf[at, here] = grad_softmax
+            total = jnp.sum(exponents, axis=0, keepdims=True)
+            inner = jnp.sum(exponents * grad_softmax, axis=0, keepdims=True)
+            if k > 0:
+                total = total + sums[0:1, here]
+                inner = inner + sums[1:2, here]
+            if k == 3:
+                total = 1.0 / total
+                inner = inner * total
+            sums[0:1, here] = total
+            sums[1:2, here] = inner
+
     to_dp(0)
     loads[0].wait()
     loads[1].wait()
     for copy in w_copies:
         copy.wait_recv()
-    loads[3].wait()
     project(0)
     for h in range(2):
         z_wait(2, h)
@@ -270,52 +313,15 @@
     y_forward(2)
     dp_forward(0)
     project(1)
+    scores_of(0)
     y_forward(3)
     dp_forward(1)
+    scores_of(1)
     project(2)
+    scores_of(2)
     project(3)
-
-    for k in range(4):
-        at = pl.ds(pl.multiple_of(a_of[k] * block, block), block)
-        remote(raw_send.at[at, :], raw_recv.at[at, :], pr_ss.at[k], pr_rs.at[k], partner).wait_recv()
-    projected = raw[...] + raw_recv[...]
-    key_raw = projected[:, :HEAD]
-    values = projected[:, HEAD:].astype(BF16)
-    key_scale = lax.rsqrt(jnp.mean(key_raw * key_raw, axis=-1, keepdims=True) + EPSILON)
-    key_normed = key_raw * key_scale
-    keys = (key_normed * k_gain).astype(BF16)
-    factor = 1.0 / math.sqrt(HEAD)
-    nt = (((1,), (1,)), ((), ()))
-    tn = (((0,), (0,)), ((), ()))
-
-    def head(h, carry):
-        grad_key, grad_value, gain = carry
-        at = pl.ds(pl.multiple_of(h * HEAD, HEAD), HEAD)
-        query = qs_buf[:, at]
-        upstream = ct_buf[:, at]
-        scores = lax.dot_general(keys, query, nt, preferred_element_type=F32) * factor
-        exponents = jnp.exp(scores) * mask[...]
-        softmax = exponents * (1.0 / jnp.sum(exponents, axis=0, keepdims=True))
-        grad_softmax = lax.dot_general(values, upstream, nt, preferred_element_type=F32)
-        inner = jnp.sum(softmax * grad_softmax, axis=0, keepdims=True)
-        grad_scores = (softmax * (grad_softmax - inner)).astype(BF16)
-        grad_value = grad_value + jnp.dot(softmax.astype(BF16), upstream, preferred_element_type=F32)
-        grad_key = grad_key + jnp.dot(grad_scores, query, preferred_element_type=F32)
-        grad_query = lax.dot_general(grad_scores, keys, tn, preferred_element_type=F32)
-        gain = gain + jnp.sum(grad_query * qn_buf[:, at], axis=0, keepdims=True)
-        return grad_key, grad_value, gain
-
-    zero = jnp.zeros((rows, HEAD), F32)
-    grad_key, grad_value, gain_query = lax.fori_loop(
-        0, heads, head, (zero, zero, jnp.zeros((1, HEAD), F32)), unroll=4
-    )
-    grad_key = grad_key * factor
-    scaled_up = grad_key * k_gain
-    key_back = key_scale * (
-        scaled_up - key_normed * jnp.mean(scaled_up * key_normed, axis=-1, keepdims=True)
-    )
-    kv[:, :HEAD] = key_back.astype(BF16)
-    kv[:, HEAD : 2 * HEAD] = grad_value.astype(BF16)
+    scores_of(3)
+
     b_of = [lax.rem(a + 2, 4), lax.rem(a + 1, 4), lax.rem(a + 3, 4), a]
     kv_to = [partner, dev(l_=mate), dev(l_=mate, c_=1 - c)]
 
@@ -324,21 +330,44 @@
         dst = kv.at[at, 2 * (i + 1) * HEAD : 2 * (i + 2) * HEAD]
         return remote(kv.at[at, : 2 * HEAD], dst, kv_ss.at[k, i], kv_rs.at[k, i], kv_to[i])
 
-    for k in range(4):
-        for i in range(3):
-            send(kv_copy(k, i))
-
-    gain_a[l] = jnp.concatenate(
-        [
-            jnp.sum(grad_key * key_normed, axis=0, keepdims=True),
-            gain_query * factor,
-            jnp.zeros((6, HEAD), F32),
-        ],
-        axis=0,
-    )
-    for d in range(1, 4):
-        to = dev(l_=lax.rem(l + d, 4))
-        send(remote(gain_a.at[l], gain_a.at[l], ga_ss.at[d - 1], ga_rs.at[d - 1], to))
+    key_gains = []
+
+    def grads():
+        at = slice(0, rows)
+        grad_key = jnp.zeros((rows, HEAD), F32)
+        grad_value = jnp.zeros((rows, HEAD), F32)
+        for start in groups:
+            here = slice(start, start + group_cols)
+            softmax = e_buf[at, here] * sums[0:1, here]
+            grad_scores = (softmax * (g_buf[at, here] - sums[1:2, here])).astype(BF16)
+            gs_buf[at, here] = grad_scores
+            grad_value += jnp.dot(softmax.astype(BF16), ct_buf[here, :], preferred_element_type=F32)
+            grad_key += jnp.dot(grad_scores, qs_buf[here, :], preferred_element_type=F32)
+        grad_key = grad_key * factor
+        key_normed = kn_buf[at, :]
+        scaled_up = grad_key * k_gain
+        key_back = ks_buf[at, :] * (
+            scaled_up - key_normed * jnp.mean(scaled_up * key_normed, axis=-1, keepdims=True)
+        )
+        kv[at, :HEAD] = key_back.astype(BF16)
+        kv[at, HEAD : 2 * HEAD] = grad_value.astype(BF16)
+        for k in range(4):
+            for i in range(3):
+                send(kv_copy(k, i))
+        key_gains.append(jnp.sum(grad_key * key_normed, axis=0, keepdims=True))
+
+    def share_gains():
+        gain_query = jnp.zeros((1, HEAD), F32)
+        for start in groups:
+            here = slice(start, start + group_cols)
+            grad_query = lax.dot_general(gs_buf[:, here], key_buf[...], tn, preferred_element_type=F32)
+            gain_query += jnp.sum(grad_query * qn_buf[here, :], axis=0, keepdims=True)
+        gain_a[l] = jnp.concatenate(
+            [sum(key_gains), gain_query * factor, jnp.zeros((6, HEAD), F32)], axis=0
+        )
+        for d in range(1, 4):
+            to = dev(l_=lax.rem(l + d, 4))
+            send(remote(gain_a.at[l], gain_a.at[l], ga_ss.at[d - 1], ga_rs.at[d - 1], to))
 
     y_up, y_down = dev(y_=y + 1), dev(y_=y - 1)
     split = quarter // 2 // HEAD * HEAD + HEAD
@@ -401,6 +430,8 @@
         copy = remote(yred.at[k], zin.at[k, slot], in_ss.at[k], in_rs.at[k, slot], to)
         send(copy, jnp.logical_not(active) if k == 3 else None)
 
+    grads()
+    share_gains()
     dp_finish()
     terms(0)
     opposite(0)
@@ -415,7 +446,6 @@
     beside(2)
     terms(3)
     opposite(3)
-
     for d in range(1, 4):
         src = gain_a.at[lax.rem(l - d + 4, 4)]
         remote(src, src, ga_ss.at[d - 1], ga_rs.at[d - 1], partner).wait_recv()
@@ -498,6 +528,7 @@
     vmem = pl.BlockSpec(memory_space=pltpu.VMEM)
     hbm = pl.BlockSpec(memory_space=pltpu.HBM)
     dma = pltpu.SemaphoreType.DMA
+    stacked = tok * q_width // HEAD
     scratch = [
         pltpu.VMEM((8, width), BF16),
         pltpu.VMEM(key_gain.shape, F32),
@@ -506,12 +537,19 @@
         pltpu.VMEM(row_doc.shape, jnp.int32),
         pltpu.VMEM((half, 4 * HEAD), BF16),
         pltpu.VMEM((quarter, 4 * HEAD), BF16),
-        pltpu.VMEM((tok, q_width), BF16),
-        pltpu.VMEM((tok, q_width), BF16),
-        pltpu.VMEM((tok, q_width), BF16),
-        pltpu.VMEM((tok, q_width), F32),
+        pltpu.VMEM((stacked, HEAD), BF16),
+        pltpu.VMEM((stacked, HEAD), BF16),
+        pltpu.VMEM((stacked, HEAD), BF16),
+        pltpu.VMEM((stacked, HEAD), F32),
         pltpu.VMEM((8, half), F32),
         pltpu.VMEM((8, half), F32),
+        pltpu.VMEM((rows, stacked), F32),
+        pltpu.VMEM((rows, stacked), F32),
+        pltpu.VMEM((rows, stacked), BF16),
+        pltpu.VMEM((8, stacked), F32),
+        pltpu.VMEM((rows, HEAD), F32),
+        pltpu.VMEM((rows, HEAD), F32),
+        pltpu.VMEM((rows, HEAD), BF16),
         pltpu.VMEM((rows, half), BF16),
         pltpu.VMEM((rows, 2 * HEAD), F32),
         pltpu.VMEM((rows, 2 * HEAD), F32),
@@ -527,10 +565,10 @@
         pltpu.VMEM((8, quarter), F32),
         pltpu.VMEM((4, 8, HEAD), F32),
         pltpu.VMEM((4, 8, HEAD), F32),
-        pltpu.VMEM((rows, tok), F32),
+        pltpu.VMEM((rows, 2 * tok), F32),
         dma((5,)), dma((2,)), dma((2,)), dma((2,)),
         dma((4,)), dma((4,)), dma((2, 2)), dma((2, 2)), dma((2,)), dma((2,)),
-        dma((2,)), dma, dma,
+        dma((2, q_width // HEAD)), dma, dma,
         dma((3, 2)), dma((2, 2)), dma((4, 2)),
         dma((4, 2, 2)), dma((4, 2, 2)), dma((4, 2)), dma((4, 2)),
         dma((4,)), dma((4,)), dma((4, 3)), dma((4, 3)),

time: 79.2 us -> 77.8 us (0.982)
  Pallas kernels: 78.3 us -> 76.7 us
    pallas_call x1, Pallas kernels: 76.3 us -> 74.6 us  [on_device(): pl.pallas_call(kernel, name='image_row_gradients', out_shape=(jax.ShapeDt...]
where the time goes in v4:
time: 77.8 us; the launch traced here: 77.4 us
  Pallas kernels  76.7 us (99%)
    pallas_call x1, Pallas kernels, on_device(): pl.pallas_call(kernel, name='image_row_gradients', out_shape=(jax.ShapeDt...  74.6 us
    pallas_call x1, Pallas kernels, on_device(): pl.pallas_call(hand_over, name='hand_over', out_shape=(jax.ShapeDtypeStru...  2.09 us

profile of v4, /device:TPU:1, one launch (start us, length us, event | category | flops | bytes accessed | tf_op | source)
XLA Modules:
  0.0 77.4 jit_solution(9179173356972598421)
XLA Ops:
  0.6 74.6 %image_row_gradients.1 = (bf16[8,1920]{1,0:T(8,128)(2,1)}, f32[1,128]{1,0:T(1,128)}, f32[1,128]{1,0:T(1,128)}) custom-call(bf16[8,7680]{1,0:T(8,128)(2,1)} %bitcast.10, bf16[7680,128]{1,0:T(8,128)(2,1)} %bitcast.6, bf16[7680,128]{1,0:T(8,128)(2,1)} %bitcast.7, f32[16,128]{1,0:T(8,128)} %kg_hbm.1, f32[16,128]{1,0:T(8,128)} %qg_hbm.1, ...), custom_call_target="tpu_custom_call" | custom-call | tf_op jit(solution)/shard_map/image_row_gradients/pallas_call | solution.py:579
  75.3 2.1 %hand_over.1 = (bf16[1,8,1920]{2,1,0:T(8,128)(2,1)}, f32[1,128]{1,0:T(1,128)}, f32[1,128]{1,0:T(1,128)}) custom-call(bf16[1,8,1920]{2,1,0:T(8,128)(2,1)} %bitcast.11, f32[1,128]{1,0:T(1,128)} %get-tuple-element.7.b_ref, f32[1,128]{1,0:T(1,128)} %get-tuple-element.8.c_ref), custom_call_target="tpu_custom_call" | custom-call | tf_op jit(solution)/shard_map/hand_over/pallas_call | solution.py:598

commit v5 on v4

--- a/solution.py
+++ b/solution.py
@@ -63,6 +63,21 @@
     step = jnp.where(even, 1, -1)
     a_of = [a, lax.rem(a - step + 4, 4), lax.rem(a + step + 4, 4), lax.rem(a + 2, 4)]
 
+    barrier = pltpu.get_barrier_semaphore()
+
+    def greet(to):
+        pl.semaphore_signal(barrier, inc=1, device_id=to, device_id_type=MESH)
+
+    greet(partner)
+    greet(dev(y_=y + 1))
+    greet(dev(y_=y - 1))
+    for d in range(1, 4):
+        greet(dev(l_=lax.rem(l + d, 4)))
+        greet(dev(x_=lax.rem(xi + d, 4)))
+
+    greet(dev(l_=mate, c_=1 - c))
+    greet(dev(a_=a - step, l_=jnp.where(even, 3, 0)))
+
     small = [
         pltpu.make_async_copy(src, dst, s_sem.at[i])
         for i, (src, dst) in enumerate(
@@ -71,21 +86,6 @@
     ]
     for copy in small:
         copy.start()
-
-    barrier = pltpu.get_barrier_semaphore()
-
-    def greet(to):
-        pl.semaphore_signal(barrier, inc=1, device_id=to, device_id_type=MESH)
-
-    greet(partner)
-    greet(dev(y_=y + 1))
-    greet(dev(y_=y - 1))
-    for d in range(1, 4):
-        greet(dev(l_=lax.rem(l + d, 4)))
-        greet(dev(x_=lax.rem(xi + d, 4)))
-
-    greet(dev(l_=mate, c_=1 - c))
-    greet(dev(a_=a - step, l_=jnp.where(even, 3, 0)))
 
     own_rows = pl.ds(pl.multiple_of(c * half, 128), half)
     their_rows = pl.ds(pl.multiple_of((1 - c) * half, 128), half)
@@ -161,9 +161,9 @@
             part_ = piece_of(xi + 2, i)
             remote(part_, part_, wf_ss.at[i], wf_rs.at[i], partner).wait_recv()
 
-    to_mate(0)
     send(remote(xs, xr, x_ss, x_rs, partner))
     x_copy = pending[-1][1]
+    to_mate(0)
     x_copy.wait_recv()
     got = xr[...]
     mine = pl.ds(pl.multiple_of((a * 4 + y) * ROWS, ROWS), ROWS)

time: 77.8 us -> 77.5 us (level)
  no operation moved by 1% of the time
where the time goes in v5:
time: 77.5 us; the launch traced here: 77.4 us
  Pallas kernels  76.7 us (99%)
    pallas_call x1, Pallas kernels, on_device(): pl.pallas_call(kernel, name='image_row_gradients', out_shape=(jax.ShapeDt...  74.6 us
    pallas_call x1, Pallas kernels, on_device(): pl.pallas_call(hand_over, name='hand_over', out_shape=(jax.ShapeDtypeStru...  2.09 us

profile of v5, /device:TPU:1, one launch (start us, length us, event | category | flops | bytes accessed | tf_op | source)
XLA Modules:
  0.0 77.4 jit_solution(5966189516346945287)
XLA Ops:
  0.6 74.6 %image_row_gradients.1 = (bf16[8,1920]{1,0:T(8,128)(2,1)}, f32[1,128]{1,0:T(1,128)}, f32[1,128]{1,0:T(1,128)}) custom-call(bf16[8,7680]{1,0:T(8,128)(2,1)} %bitcast.10, bf16[7680,128]{1,0:T(8,128)(2,1)} %bitcast.6, bf16[7680,128]{1,0:T(8,128)(2,1)} %bitcast.7, f32[16,128]{1,0:T(8,128)} %kg_hbm.1, f32[16,128]{1,0:T(8,128)} %qg_hbm.1, ...), custom_call_target="tpu_custom_call" | custom-call | tf_op jit(solution)/shard_map/image_row_gradients/pallas_call | solution.py:579
  75.3 2.1 %hand_over.1 = (bf16[1,8,1920]{2,1,0:T(8,128)(2,1)}, f32[1,128]{1,0:T(1,128)}, f32[1,128]{1,0:T(1,128)}) custom-call(bf16[1,8,1920]{2,1,0:T(8,128)(2,1)} %bitcast.11, f32[1,128]{1,0:T(1,128)} %get-tuple-element.7.b_ref, f32[1,128]{1,0:T(1,128)} %get-tuple-element.8.c_ref), custom_call_target="tpu_custom_call" | custom-call | tf_op jit(solution)/shard_map/hand_over/pallas_call | solution.py:598
